TPU v7x, 32 devices: a whole 2x2x4 slice. The times are simulated.
32 devices in a mesh: seq: 16 (over z, x, core), fsdp: 2 (over y).
Axes of the slice: x: 2, y: 2, z: 4, core: 2. Of those that a mesh axis runs over, the one named last changes fastest.
Arguments:
- tokens: bfloat16 [8192, 640], P(('seq', 'fsdp')), may hold values from -6 to 6
- positions: int32 [8192], P(('seq', 'fsdp')), may hold values from 0 to 7935, as said below
- cotangent: bfloat16 [8192, 640], P(('seq', 'fsdp')), may hold values from -6 to 6
- in_gain: bfloat16 [640], P('fsdp'), may hold values from 0.25 to 1.75
- w_query: bfloat16 [640, 1024], P('fsdp'), may hold values from -0.25 to 0.25
- w_key: bfloat16 [640, 256], P('fsdp'), may hold values from -0.25 to 0.25
- w_value: bfloat16 [640, 256], P('fsdp'), may hold values from -0.25 to 0.25
- query_gain: bfloat16 [256], P('fsdp'), may hold values from 0.25 to 1.75
- key_gain: bfloat16 [256], P('fsdp'), may hold values from 0.25 to 1.75
- w_out: bfloat16 [1024, 640], P('fsdp'), may hold values from -0.1875 to 0.1875
- attn_gain: bfloat16 [640], P('fsdp'), may hold values from 0.25 to 1.75
- ffn_gain_in: bfloat16 [640], P('fsdp'), may hold values from 0.25 to 1.75
- w_gate: bfloat16 [640, 2048], P('fsdp'), may hold values from -0.25 to 0.25
- w_up: bfloat16 [640, 2048], P('fsdp'), may hold values from -0.25 to 0.25
- w_down: bfloat16 [2048, 640], P('fsdp'), may hold values from -0.125 to 0.125
- ffn_gain_out: bfloat16 [640], P('fsdp'), may hold values from 0.25 to 1.75
Outputs:
- layer_out: bfloat16 [8192, 640], P(('seq', 'fsdp'))
- grad_tokens: float32 [8192, 640], P(('seq', 'fsdp'))
- grad_in_gain: float32 [640], P('fsdp')
- grad_query: float32 [640, 1024], P('fsdp')
- grad_key: float32 [640, 256], P('fsdp')
- grad_value: float32 [640, 256], P('fsdp')
- grad_query_gain: float32 [256], P('fsdp')
- grad_key_gain: float32 [256], P('fsdp')
- grad_w_out: float32 [1024, 640], P('fsdp')
- grad_attn_gain: float32 [640], P('fsdp')
- grad_ffn_gain_in: float32 [640], P('fsdp')
- grad_gate: float32 [640, 2048], P('fsdp')
- grad_up: float32 [640, 2048], P('fsdp')
- grad_down: float32 [2048, 640], P('fsdp')
- grad_ffn_gain_out: float32 [640], P('fsdp')
Inputs may be any that keep to these rules, and one draw needn't show every extreme that they name: Sequences lie end to end: one holds 7936 tokens and begins within the first 256 tokens; the others, before and after it, hold 256 tokens together; positions count from 0 in each sequence.
All inputs are finite; a program needn't handle non-finite values.
Results may differ from a plain program's by a relative error of at most 0.017.
Values may be sent and summed in bfloat16 or wider, within the bound.
No kernel may reach another device: no remote copies, remote signals or barrier semaphores. Data moves between devices by JAX's collectives and lax.ppermute only.
A program may use at most 128 MiB of HBM per device.

v0:
```python
import functools
import math

import jax
import jax.numpy as jnp
from jax import lax
from jax.experimental import pallas as pl
from jax.experimental.pallas import tpu as pltpu
from jax.sharding import PartitionSpec as P

WINDOW = 512
EPSILON = 1e-06
ROPE_BASE = 10000.0
MASKED = -1e30
BF16 = jnp.bfloat16
F32 = jnp.float32
QBLOCK = 128
LANES = 128
GAIN_ROWS = 32
GELU_A = math.sqrt(2.0 / math.pi)
GELU_B = 0.044715

VMEM = pl.BlockSpec(memory_space=pltpu.VMEM)
SMEM = pl.BlockSpec(memory_space=pltpu.SMEM)
ANY = pl.BlockSpec(memory_space=pl.ANY)


def wrapped(value, size):
    return value & (size - 1) if size & (size - 1) == 0 else lax.rem(value, jnp.int32(size))


class Places:
    def __init__(self):
        self.seq = lax.axis_size("seq")
        self.fsdp = lax.axis_size("fsdp")
        self.outer = self.seq // 4
        index = lax.axis_index("seq").astype(jnp.int32)
        fsdp_at = lax.axis_index("fsdp").astype(jnp.int32)
        outer_at = lax.shift_right_logical(index, 2)
        core_at, mid_at = index & 1, lax.shift_right_logical(index, 1) & 1
        scalars = lax.optimization_barrier(
            (
                core_at,
                mid_at,
                fsdp_at,
                core_at * 2 + mid_at,
                tuple(wrapped(outer_at + by, self.outer) for by in range(self.outer)),
                tuple(wrapped(outer_at - by + self.outer, self.outer) for by in range(self.outer)),
                tuple(wrapped(fsdp_at + by, self.fsdp) for by in range(self.fsdp)),
                tuple(wrapped(fsdp_at - by + self.fsdp, self.fsdp) for by in range(self.fsdp)),
                jnp.stack([core_at, mid_at, fsdp_at]),
            )
        )
        self.core_at, self.mid_at, self.fsdp_at, self.quarter_at = scalars[:4]
        self.outer_ahead, self.outer_behind, self.fsdp_ahead, self.fsdp_behind, self.vector = scalars[4:]

    def core_swap(self, array):
        return lax.ppermute(array, "seq", [(i, i ^ 1) for i in range(self.seq)])

    def mid_swap(self, array):
        return lax.ppermute(array, "seq", [(i, i ^ 2) for i in range(self.seq)])

    def outer_shift(self, array, by):
        return lax.ppermute(array, "seq", [(i, (i + 4 * by) % self.seq) for i in range(self.seq)])

    def fsdp_shift(self, array, by):
        return lax.ppermute(array, "fsdp", [(i, (i + by) % self.fsdp) for i in range(self.fsdp)])


def linear_shift(array, by):
    count = lax.axis_size("seq") * lax.axis_size("fsdp")
    return lax.ppermute(array, ("seq", "fsdp"), [(i, i + by) for i in range(count) if 0 <= i + by < count])


def pick(array, at):
    return lax.dynamic_index_in_dim(array, at, 0, keepdims=False, allow_negative_indices=False)


def ordered(pieces, behind):
    if len(pieces) == 2:
        own, other = pieces
        return jnp.where(behind[0] == 0, jnp.stack([own, other]), jnp.stack([other, own]))
    stacked = jnp.stack(pieces)
    return jnp.stack([pick(stacked, at) for at in behind])


def own_part(here, shards, axis, ways):
    size = sum(shard.shape[axis] for shard in shards) // ways
    place = here.quarter_at if ways == 4 else here.core_at
    if len(shards) == 1:
        return lax.dynamic_slice_in_dim(shards[0], place * size, size, axis, allow_negative_indices=False)
    parts = []
    for i in range(ways):
        pieces, start = [], 0
        for shard in shards:
            low, high = max(i * size - start, 0), min((i + 1) * size - start, shard.shape[axis])
            if low < high:
                pieces.append(lax.slice_in_dim(shard, low, high, axis=axis))
            start += shard.shape[axis]
        parts.append(jnp.concatenate(pieces, axis))
    return functools.reduce(lambda rest, i: jnp.where(place == i, parts[i], rest), range(1, ways), parts[0])


def after(value, *earlier):
    return lax.optimization_barrier((value, *earlier))[0]


def together(*groups):
    return lax.optimization_barrier(tuple(tuple(group) for group in groups))


def over_links(here, part):
    return [here.fsdp_shift(part, by) for by in range(1, here.fsdp)]


def on_chips(here, arrived, ways):
    pieces = []
    for mine in arrived:
        if ways == 4:
            across = here.mid_swap(mine)
            pieces += [mine, across, here.core_swap(mine), here.core_swap(across)]
        else:
            pieces += [mine, here.core_swap(mine)]
    return pieces


def multiple(value, of):
    return pl.multiple_of(value, of)


def place_copies(owned, pieces, whole, sems, at, axis, ways):
    core, mid, fsdp = at[0], at[1], at[2]
    count = 1 + len(pieces) // ways
    rows = owned[0].shape[0]
    copies = []
    column = 0
    own_row = multiple(fsdp * rows, 16)
    for shard in owned:
        wide = shard.shape[1]
        copies.append((shard, whole.at[pl.ds(own_row, rows), pl.ds(column, wide)]))
        column += wide
    for k, piece in enumerate(pieces):
        by = 1 + k // ways
        row = multiple(lax.rem(fsdp + (count - by), count) * rows, 16)
        k = k % ways
        if ways == 4:
            place = (core if k < 2 else 1 - core) * 2 + (mid if k % 2 == 0 else 1 - mid)
        else:
            place = core if k == 0 else 1 - core
        if axis == 0:
            target = whole.at[pl.ds(multiple(row + place * (rows // ways), 16), rows // ways), :]
        else:
            target = whole.at[pl.ds(row, rows), pl.ds(multiple(place * (column // ways), 128), column // ways)]
        copies.append((piece, target))
    return [pltpu.make_async_copy(a, b, sems.at[k]) for k, (a, b) in enumerate(copies)]


def dot(a, b):
    return lax.dot_general(a, b, (((1,), (0,)), ((), ())), preferred_element_type=F32)


def dot_nt(a, b):
    return lax.dot_general(a, b, (((1,), (1,)), ((), ())), preferred_element_type=F32)


def dot_tn(a, b):
    return lax.dot_general(a, b, (((0,), (0,)), ((), ())), preferred_element_type=F32)


def inverse_rms(u):
    return lax.rsqrt(jnp.mean(u * u, axis=-1, keepdims=True) + EPSILON)


def norm_back(u, g, dz):
    r = inverse_rms(u)
    ur = u * r
    gdz = g * dz
    du = r * (gdz - ur * jnp.mean(gdz * ur, axis=-1, keepdims=True))
    return du, jnp.sum(dz * ur, axis=0, keepdims=True)


class Writer:
    def __init__(self, sems):
        self.sems, self.copies = sems, []

    def put(self, source, target):
        copy = pltpu.make_async_copy(source, target, self.sems.at[len(self.copies)])
        copy.start()
        self.copies.append(copy)

    def wait(self):
        for copy in self.copies:
            copy.wait()


def params(megabytes=56):
    return pltpu.CompilerParams(vmem_limit_bytes=megabytes * 1024 * 1024)


def cost(flops, bytes_accessed):
    return pl.CostEstimate(flops=int(20 * flops), bytes_accessed=int(20 * bytes_accessed), transcendentals=0)


def shape(dims, kind):
    return jax.ShapeDtypeStruct(tuple(dims), kind)


def attend_kernel(n_tok, n_qkv, heads, *refs):
    at = refs[0]
    toks = refs[1 : 1 + n_tok]
    pos, cosine, sine, gain_table = refs[1 + n_tok : 5 + n_tok]
    qkv = refs[5 + n_tok : 5 + n_tok + n_qkv]
    normed, q_raw, k_raw, q_st, keys, values, probs, attended, w_full, sems = refs[5 + n_tok + n_qkv :]
    copies = place_copies(qkv[:3], qkv[3:], w_full, sems, at, 1, 4)
    for copy in copies:
        copy.start()
    rows = toks[0].shape[0]
    dim = keys.shape[1]
    half = dim // 2
    halo = (n_tok - 1) * rows
    gain = gain_table[0:1, :]
    gain_q, gain_k = gain_table[1:2, :dim], gain_table[2:3, :dim]
    for i, tok in enumerate(toks):
        u = tok[...].astype(F32)
        normed[i * rows : (i + 1) * rows, :] = (u * inverse_rms(u) * gain).astype(BF16)
    for copy in copies:
        copy.wait()

    def turned(u, g, cos, sin):
        u = u * inverse_rms(u) * g
        first, second = u[:, :half], u[:, half:]
        return (first * cos - second * sin).astype(BF16), (second * cos + first * sin).astype(BF16)

    for i in range(n_tok):
        here = slice(i * rows, (i + 1) * rows)
        kv = dot(normed[here, :], w_full[:, heads * dim :])
        k_raw[here, :] = kv[:, :dim]
        values[here, :] = kv[:, dim:].astype(BF16)
        first, second = turned(kv[:, :dim], gain_k, cosine[here, :], sine[here, :])
        keys[here, :half] = first
        keys[here, half:] = second
    blocks = rows // QBLOCK
    for h in range(heads):
        u = dot(normed[halo:, :], w_full[:, h * dim : (h + 1) * dim])
        q_raw[:, h * dim : (h + 1) * dim] = u
        first, second = turned(u, gain_q, cosine[halo:, :], sine[halo:, :])
        for b in range(blocks):
            start = (b * heads + h) * QBLOCK
            q_st[start : start + QBLOCK, :half] = first[b * QBLOCK : (b + 1) * QBLOCK, :]
            q_st[start : start + QBLOCK, half:] = second[b * QBLOCK : (b + 1) * QBLOCK, :]
    span = WINDOW + QBLOCK
    distance = (
        lax.broadcasted_iota(jnp.int32, (QBLOCK, span), 0)
        + WINDOW
        - lax.broadcasted_iota(jnp.int32, (QBLOCK, span), 1)
    )
    scale = dim ** (-0.5)
    for b in range(blocks):
        first_key = halo - WINDOW + b * QBLOCK
        limit = jnp.minimum(pos[b * QBLOCK : (b + 1) * QBLOCK, :], WINDOW - 1)
        allowed = (distance >= 0) & (distance <= limit)
        for h in range(heads):
            start = (b * heads + h) * QBLOCK
            scores = dot_nt(q_st[start : start + QBLOCK, :], keys[first_key : first_key + span, :]) * scale
            scores = jnp.where(allowed, scores, MASKED)
            weights = jnp.exp(scores - jnp.max(scores, axis=-1, keepdims=True))
            weights = (weights * (1.0 / jnp.sum(weights, axis=-1, keepdims=True))).astype(BF16)
            probs[start : start + QBLOCK, :] = weights
            attended[b * QBLOCK : (b + 1) * QBLOCK, h * dim : (h + 1) * dim] = dot(
                weights, values[first_key : first_key + span, :]
            ).astype(BF16)


def gate_kernel(n_out, n_gate, n_up, *refs):
    at, attended, tokens, gain_table = refs[:4]
    refs = refs[4:]
    out_w, gate_w, up_w, refs = (
        refs[:n_out],
        refs[n_out : n_out + n_gate],
        refs[n_out + n_gate : n_out + n_gate + n_up],
        refs[n_out + n_gate + n_up :],
    )
    projected_out, residual_out, ffn_in_ref, mixed_out, gelu_out_out, gate_slope_out = refs[:6]
    (
        projected_ref, residual_ref, mixed, gelu_out, gate_slope,
        out_full, gate_full, up_full, out_sems, gate_sems, up_sems, write_sems,
    ) = refs[6:]
    writer = Writer(write_sems)
    groups = (
        place_copies(out_w[:1], out_w[1:], out_full, out_sems, at, 0, 2),
        place_copies(gate_w[:1], gate_w[1:], gate_full, gate_sems, at, 1, 4),
        place_copies(up_w[:1], up_w[1:], up_full, up_sems, at, 1, 2),
    )
    for group in groups:
        for copy in group:
            copy.start()
    for copy in groups[0]:
        copy.wait()
    projected = dot(attended[...], out_full[...])
    projected_ref[...] = projected
    residual = tokens[...].astype(F32) + projected * inverse_rms(projected) * gain_table[3:4, :]
    residual_ref[...] = residual
    ffn_in_ref[...] = (residual * inverse_rms(residual) * gain_table[4:5, :]).astype(BF16)
    writer.put(projected_ref, projected_out)
    writer.put(residual_ref, residual_out)
    width = gate_full.shape[1] // 4
    for k in range(4):
        waits = groups[1][1 + k :: 4] + (groups[2][1 + k // 2 :: 2] if k % 2 == 0 else [])
        if k == 0:
            waits = groups[1][:1] + groups[2][:1] + waits
        for copy in waits:
            copy.wait()
        core = at[0] if k < 2 else 1 - at[0]
        mid = at[1] if k % 2 == 0 else 1 - at[1]
        cut = pl.ds(multiple((core * 2 + mid) * width, width), width)
        gate = dot(ffn_in_ref[...], gate_full[:, cut])
        up = dot(ffn_in_ref[...], up_full[:, cut])
        square = gate * gate
        t = jnp.tanh(GELU_A * gate * (1.0 + GELU_B * square))
        cdf = 0.5 * (1.0 + t)
        act = gate * cdf
        slope = cdf + 0.5 * gate * (1.0 - t * t) * (GELU_A * (1.0 + 3.0 * GELU_B * square))
        mixed[:, cut] = (act * up).astype(BF16)
        gelu_out[:, cut] = act.astype(BF16)
        gate_slope[:, cut] = (up * slope).astype(BF16)
        writer.put(mixed.at[:, cut], mixed_out.at[:, cut])
        writer.put(gelu_out.at[:, cut], gelu_out_out.at[:, cut])
        writer.put(gate_slope.at[:, cut], gate_slope_out.at[:, cut])
    writer.wait()


def relative_blocks(at, fsdp):
    for c in range(2):
        core = c + at[0] - 2 * c * at[0]
        for f in range(fsdp):
            row = lax.rem(at[2] + f, fsdp)
            for x in range(2):
                mid = x + at[1] - 2 * x * at[1]
                yield c, f, x, core, row, mid


def column_blocks(at, fsdp, left_t, right, keep, send):
    tall, wide = left_t.shape[0] // fsdp, keep.shape[3]
    for c, f, x, core, row, mid in relative_blocks(at, fsdp):
        cut = pl.ds(multiple((core * 2 + mid) * wide, 128), wide)
        left = left_t[pl.ds(multiple(row * tall, 16), tall), :]
        target = keep if c == 0 else send
        target[f, x, :tall, :] = dot(left, right[:, cut]).astype(BF16)


def down_kernel(n_down, fsdp, *refs):
    at, mixed, residual, cotangent, gain_table = refs[:5]
    down_w = refs[5 : 5 + n_down]
    layer_out, d_down, grad_gain, keep, send = refs[5 + n_down : 10 + n_down]
    down_full, mixed_t, sems = refs[10 + n_down :]
    copies = place_copies(down_w[:1], down_w[1:], down_full, sems, at, 0, 2)
    for copy in copies:
        copy.start()
    mixed_t[...] = mixed[...].T
    for copy in copies:
        copy.wait()
    down = dot(mixed[...], down_full[...])
    r = inverse_rms(down)
    gain = gain_table[5:6, :]
    layer_out[...] = (residual[...] + down * r * gain).astype(BF16)
    du, dg = norm_back(down, gain, cotangent[...].astype(F32))
    grad_gain[...] = dg
    d_down[...] = du.astype(BF16)
    block = keep.shape[2]
    for c, f, x, core, row, mid in relative_blocks(at, fsdp):
        start = multiple(((row * 2 + core) * 2 + mid) * block, 16)
        target = keep if c == 0 else send
        target[f, x] = dot(mixed_t[pl.ds(start, block), :], d_down[...]).astype(BF16)


def gate_back_kernel(n_down, fsdp, *refs):
    at, d_down, gelu_out, gate_slope, ffn_in = refs[:5]
    down_w = refs[5 : 5 + n_down]
    d_gate, d_up, keep, send, up_keep, up_send = refs[5 + n_down : 11 + n_down]
    down_full, ffn_t, sems = refs[11 + n_down :]
    copies = place_copies(down_w[:1], down_w[1:], down_full, sems, at, 0, 2)
    for copy in copies:
        copy.start()
    ffn_t[...] = ffn_in[...].T
    for copy in copies:
        copy.wait()
    width = 256

    def step(i, _):
        cut = pl.ds(multiple(i * width, width), width)
        d_mixed = dot_nt(d_down[...], down_full[cut, :])
        d_gate[:, cut] = (d_mixed * gate_slope[:, cut].astype(F32)).astype(BF16)
        d_up[:, cut] = (d_mixed * gelu_out[:, cut].astype(F32)).astype(BF16)
        return 0

    lax.fori_loop(0, d_gate.shape[1] // width, step, 0)
    column_blocks(at, fsdp, ffn_t, d_gate, keep, send)
    column_blocks(at, fsdp, ffn_t, d_up, up_keep, up_send)


def middle_kernel(n_out, n_gate, n_up, fsdp, heads, *refs):
    at, d_gate, d_up, residual, projected, cotangent, gain_table, attended = refs[:8]
    refs = refs[8:]
    out_w, gate_w, up_w, refs = (
        refs[:n_out],
        refs[n_out : n_out + n_gate],
        refs[n_out + n_gate : n_out + n_gate + n_up],
        refs[n_out + n_gate + n_up :],
    )
    d_residual_ref, g_ffn, g_attn, d_att, keep, send = refs[:6]
    out_full, gate_full, up_full, att_t, out_sems, gate_sems, up_sems = refs[6:]
    groups = (
        place_copies(gate_w[:1], gate_w[1:], gate_full, gate_sems, at, 1, 4),
        place_copies(up_w[:1], up_w[1:], up_full, up_sems, at, 1, 2),
        place_copies(out_w[:1], out_w[1:], out_full, out_sems, at, 0, 2),
    )
    for group in groups:
        for copy in group:
            copy.start()
    att_t[...] = attended[...].T
    for copy in groups[0]:
        copy.wait()
    d_ffn_in = dot_nt(d_gate[...], gate_full[...])
    for copy in groups[1]:
        copy.wait()
    d_ffn_in = d_ffn_in + dot_nt(d_up[...], up_full[...])
    du, dg = norm_back(residual[...], gain_table[4:5, :], d_ffn_in)
    g_ffn[...] = dg
    d_residual = cotangent[...].astype(F32) + du
    d_residual_ref[...] = d_residual
    du, dg = norm_back(projected[...], gain_table[3:4, :], d_residual)
    g_attn[...] = dg
    d_proj = du.astype(BF16)
    rows, dim = d_proj.shape[0], d_att.shape[1]
    for copy in groups[2]:
        copy.wait()
    for h in range(heads):
        part = dot_nt(d_proj, out_full[h * dim : (h + 1) * dim, :]).astype(BF16)
        for b in range(rows // QBLOCK):
            start = (b * heads + h) * QBLOCK
            d_att[start : start + QBLOCK, :] = part[b * QBLOCK : (b + 1) * QBLOCK, :]
    block = att_t.shape[0] // (4 * fsdp)
    wide = keep.shape[3]
    parts = wide // LANES
    deep = block // parts
    for c, f, x, core, row, mid in relative_blocks(at, fsdp):
        start = multiple(((row * 2 + core) * 2 + mid) * block, 16)
        part = dot(att_t[pl.ds(start, block), :], d_proj).astype(BF16)
        target = keep if c == 0 else send
        target[f, x, :block, :] = part[:, :wide]
        for i in range(parts):
            target[f, x, block:, i * LANES : (i + 1) * LANES] = part[i * deep : (i + 1) * deep, wide:]


def attend_back_kernel(halo, heads, d_att, q_st, keys, values, probs, d_q, d_k, d_v, d_scores):
    rows = d_q.shape[0]
    dim = keys.shape[1]
    blocks = rows // QBLOCK
    span = WINDOW + QBLOCK
    scale = dim ** (-0.5)
    d_k[...] = jnp.zeros(d_k.shape, F32)
    d_v[...] = jnp.zeros(d_v.shape, F32)
    for b in range(blocks):
        first_key = halo - WINDOW + b * QBLOCK
        here = slice(first_key, first_key + span)
        for h in range(heads):
            start = (b * heads + h) * QBLOCK
            stack = slice(start, start + QBLOCK)
            d_probs = dot_nt(d_att[stack, :], values[here, :])
            p = probs[stack, :].astype(F32)
            row_terms = jnp.sum(p * d_probs, axis=-1, keepdims=True)
            ds = (p * (d_probs - row_terms) * scale).astype(BF16)
            d_scores[h * QBLOCK : (h + 1) * QBLOCK, :] = ds
            d_q[b * QBLOCK : (b + 1) * QBLOCK, h * dim : (h + 1) * dim] = dot(ds, keys[here, :])
        stack = slice(b * heads * QBLOCK, (b + 1) * heads * QBLOCK)
        d_k[here, :] += dot_tn(d_scores[...], q_st[stack, :])
        d_v[here, :] += dot_tn(probs[stack, :], d_att[stack, :])


def last_kernel(n_qkv, n_tok, fsdp, heads, *refs):
    (
        at, d_residual, d_q, d_k, d_v,
        q_raw, k_raw, cosine, sine, gain_table, normed, g_ffn, g_attn, g_out,
    ) = refs[:14]
    toks = refs[14 : 14 + n_tok]
    refs = refs[14 + n_tok :]
    qkv_w, refs = refs[:n_qkv], refs[n_qkv:]
    grad_tokens, d_halo, keep, send = refs[:4]
    w_full, normed_t, d_qkv, gain_rows, qkv_sems = refs[4:]
    copies = place_copies(qkv_w[:3], qkv_w[3:], w_full, qkv_sems, at, 1, 4)
    for copy in copies:
        copy.start()
    normed_t[...] = normed[...].T
    rows = toks[0].shape[0]
    halo = (n_tok - 1) * rows
    dim = k_raw.shape[1]
    gain_in, gain_q, gain_k = gain_table[0:1, :], gain_table[1:2, :dim], gain_table[2:3, :dim]
    half = dim // 2
    tall, wide = normed_t.shape[0] // fsdp, keep.shape[3]
    def turned_back(u, g, dz, cos, sin):
        first, second = dz[:, :half], dz[:, half:]
        dz = jnp.concatenate([first * cos + second * sin, second * cos - first * sin], axis=1)
        return norm_back(u, g, dz)

    total_q = jnp.zeros((1, dim), F32)
    if halo:
        d_qkv[:halo, : heads * dim] = jnp.zeros((halo, heads * dim), BF16)
    for h in range(heads):
        cut = slice(h * dim, (h + 1) * dim)
        du, dg = turned_back(q_raw[:, cut], gain_q, d_q[:, cut], cosine[halo:, :], sine[halo:, :])
        total_q += dg
        d_qkv[halo:, cut] = du.astype(BF16)
    total_k = jnp.zeros((1, dim), F32)
    for i in range(n_tok):
        here = slice(i * rows, (i + 1) * rows)
        du, dg = turned_back(k_raw[here, :], gain_k, d_k[here, :], cosine[here, :], sine[here, :])
        total_k += dg
        d_qkv[here, heads * dim : (heads + 1) * dim] = du.astype(BF16)
        d_qkv[here, (heads + 1) * dim :] = d_v[here, :].astype(BF16)
    column_blocks(at, fsdp, normed_t, d_qkv, keep, send)
    for copy in copies:
        copy.wait()
    total_in = jnp.zeros(gain_in.shape, F32)
    for i in range(n_tok):
        here = slice(i * rows, (i + 1) * rows)
        if i < n_tok - 1:
            d_normed = dot_nt(d_qkv[here, heads * dim :], w_full[:, heads * dim :])
        else:
            d_normed = dot_nt(d_qkv[here, :], w_full[...])
        du, dg = norm_back(toks[i][...].astype(F32), gain_in, d_normed)
        total_in += dg
        if i < n_tok - 1:
            d_halo[here, :] = du.astype(BF16)
        else:
            grad_tokens[...] = d_residual[...] + du
    gain_rows[...] = jnp.zeros(gain_rows.shape, F32)
    at_row = 0
    for total in (total_in, total_q, total_k, g_attn[...], g_ffn[...], g_out[...]):
        for i in range(total.shape[1] // LANES):
            gain_rows[at_row : at_row + 1, :LANES] = total[:, i * LANES : (i + 1) * LANES]
            at_row += 1
    packed = gain_rows[...].astype(BF16)
    for target in (keep, send):
        for f in range(fsdp):
            for x in range(2):
                target[f, x, tall:, :] = packed


def add(*terms):
    out = terms[0].astype(F32)
    for term in terms[1:]:
        out = out + term.astype(F32)
    return out


class Chunk:
    def __init__(self, here, keep, send):
        self.here, self.keep = here, keep
        self.other = here.core_swap(send)

    def over_fsdp(self, *earlier):
        here = self.here
        parts = [add(self.keep[by], self.other[by]).astype(BF16) for by in range(1, here.fsdp)]
        self.arrived = [here.fsdp_shift(after(part, *earlier), by + 1) for by, part in enumerate(parts)]

    def over_mid(self, *earlier):
        self.arrived = [after(a, *earlier) for a in self.arrived]
        terms = [self.keep[0, 1], self.other[0, 1]] + [a[1] for a in self.arrived]
        self.across = self.here.mid_swap(add(*terms).astype(BF16))
        self.mine = [self.keep[0, 0], self.other[0, 0]] + [a[0] for a in self.arrived]
        return self.arrived[0] if self.arrived else self.other

    def join(self, below, *earlier):
        for chunk in (self, below):
            chunk.arrived = [after(a, *earlier) for a in chunk.arrived]
        pairs = [
            [[c.keep[0, x], c.other[0, x]] + [a[x] for a in c.arrived] for c in (self, below)] for x in range(2)
        ]
        self.across_sent = jnp.concatenate([add(*terms).astype(BF16) for terms in pairs[1]])
        self.across = self.here.mid_swap(self.across_sent)
        self.mine = [jnp.concatenate([add(*terms).astype(BF16) for terms in pairs[0]])]

    def outer_sums(self, *earlier):
        here = self.here
        self.across = after(self.across, *earlier)
        mine = add(*self.mine, self.across).astype(BF16)
        n, w = mine.shape
        mine = mine.reshape(here.outer, n // here.outer, w)
        self.shares = [pick(mine, here.outer_ahead[0])]
        for by in range(1, here.outer):
            self.shares.append(here.outer_shift(pick(mine, here.outer_ahead[by]), by))
        return self.across

    def outer_gather(self, *earlier):
        here = self.here
        self.shares = list(after(tuple(self.shares), *earlier))
        own = add(*self.shares).astype(BF16)
        self.gathered = [own] + [here.outer_shift(own, by) for by in range(1, here.outer)]
        return self.shares[-1]

    def mid_gather(self, *earlier):
        here = self.here
        self.gathered = list(after(tuple(self.gathered), *earlier))
        block = ordered(self.gathered, here.outer_behind)
        block = block.reshape(-1, block.shape[-1])
        across = here.mid_swap(block)
        self.blocks = [[block, across], [here.core_swap(block), here.core_swap(across)]]
        return self.gathered[-1]


def by_place(here, blocks):
    own = [jnp.where(here.mid_at == 0, a, b) for a, b in blocks]
    other = [jnp.where(here.mid_at == 0, b, a) for a, b in blocks]
    pairs = list(zip(own, other))
    first = [jnp.where(here.core_at == 0, a, b) for a, b in zip(pairs[0], pairs[1])]
    second = [jnp.where(here.core_at == 0, b, a) for a, b in zip(pairs[0], pairs[1])]
    return first + second


def last_columns(blocks, start, count):
    wide = blocks[0].shape[1]
    pieces = []
    for i, block in enumerate(blocks):
        low, high = max(start - i * wide, 0), min(start + count - i * wide, wide)
        if low < high:
            pieces.append(block[:, low:high])
    return jnp.concatenate(pieces, axis=1).astype(F32)


def on_device(
    tokens, positions, cotangent, in_gain, w_query, w_key, w_value, query_gain, key_gain, w_out, attn_gain,
    ffn_gain_in, w_gate, w_up, w_down, ffn_gain_out,
):
    here = Places()
    fsdp = here.fsdp
    rows, width = tokens.shape
    dim = w_key.shape[1]
    query_cols = w_query.shape[1]
    heads = query_cols // dim
    hidden = w_gate.shape[1]
    hops = (WINDOW + rows - 1) // rows
    n_tok = hops + 1
    halo = hops * rows
    every = halo + rows
    at = here.vector

    gains = (in_gain, query_gain, key_gain, attn_gain, ffn_gain_in, ffn_gain_out)
    cuts = [0]
    for gain in gains:
        cuts.append(cuts[-1] + gain.shape[0])
    gain_row = jnp.concatenate(gains)
    gain_rows = ordered([gain_row] + [here.fsdp_shift(gain_row, by) for by in range(1, fsdp)], here.fsdp_behind)
    gain_rows = gain_rows.astype(F32)
    gain_table = jnp.concatenate(
        [
            jnp.pad(gain_rows[:, cuts[i] : cuts[i + 1]].reshape(1, -1), ((0, 0), (0, width - fsdp * gains[i].shape[0])))
            for i in range(6)
        ]
        + [jnp.zeros((2, width), F32)],
        axis=0,
    )
    qkv_w = [w_query, w_key, w_value]
    qkv_part = own_part(here, qkv_w, 1, 4)
    tokens_out = after(tokens, qkv_part)
    toks = [linear_shift(tokens_out, by) for by in range(hops, 0, -1)] + [tokens]
    qkv_w += on_chips(here, over_links(here, qkv_part), 4)
    out_arrived = over_links(here, after(own_part(here, [w_out], 0, 2), *toks[:-1]))
    gate_arrived = over_links(here, after(own_part(here, [w_gate], 1, 4), qkv_w[3]))
    up_arrived = over_links(here, after(own_part(here, [w_up], 1, 2), *gate_arrived))
    down_arrived = over_links(here, after(own_part(here, [w_down], 0, 2), *gate_arrived))

    all_positions = jnp.concatenate([positions[0] - halo + jnp.arange(halo, dtype=jnp.int32), positions])
    frequency = ROPE_BASE ** (-(jnp.arange(dim // 2, dtype=F32) * 2.0 / dim))
    angles = all_positions.astype(F32)[:, None] * frequency[None, :]
    cosine, sine = jnp.cos(angles), jnp.sin(angles)

    span = WINDOW + QBLOCK
    weight_bytes = 2 * fsdp * w_gate.size
    normed, q_raw, k_raw, q_st, keys, values, probs, attended = pl.pallas_call(
        functools.partial(attend_kernel, n_tok, len(qkv_w), heads),
        out_shape=(
            shape((every, width), BF16),
            shape((rows, query_cols), F32),
            shape((every, dim), F32),
            shape((heads * rows, dim), BF16),
            shape((every, dim), BF16),
            shape((every, dim), BF16),
            shape((heads * rows, span), BF16),
            shape((rows, query_cols), BF16),
        ),
        in_specs=[SMEM] + [VMEM] * (n_tok + 4) + [ANY] * len(qkv_w),
        out_specs=(VMEM,) * 8,
        scratch_shapes=[
            pltpu.VMEM((width, query_cols + 2 * dim), BF16),
            pltpu.SemaphoreType.DMA((len(qkv_w),)),
        ],
        compiler_params=params(),
        cost_estimate=cost(4e9, 1e7),
        name="attend",
    )(at, *toks, after(positions[:, None], *gate_arrived), cosine, sine, gain_table, *qkv_w)

    out_w = [w_out] + on_chips(here, [after(a, attended) for a in out_arrived], 2)
    gate_w = [w_gate] + on_chips(here, gate_arrived, 4)
    up_w = [w_up] + on_chips(here, [after(a, attended) for a in up_arrived], 2)
    projected, residual, ffn_in, mixed, gelu_out, gate_slope = pl.pallas_call(
        functools.partial(gate_kernel, len(out_w), len(gate_w), len(up_w)),
        out_shape=(
            shape((rows, width), F32),
            shape((rows, width), F32),
            shape((rows, width), BF16),
            shape((rows, hidden), BF16),
            shape((rows, hidden), BF16),
            shape((rows, hidden), BF16),
        ),
        in_specs=[SMEM] + [VMEM] * 3 + [ANY] * (len(out_w) + len(gate_w) + len(up_w)),
        out_specs=(ANY, ANY, VMEM, ANY, ANY, ANY),
        scratch_shapes=[
            pltpu.VMEM((rows, width), F32),
            pltpu.VMEM((rows, width), F32),
            pltpu.VMEM((rows, hidden), BF16),
            pltpu.VMEM((rows, hidden), BF16),
            pltpu.VMEM((rows, hidden), BF16),
            pltpu.VMEM((query_cols, width), BF16),
            pltpu.VMEM((width, hidden), BF16),
            pltpu.VMEM((width, hidden), BF16),
            pltpu.SemaphoreType.DMA((len(out_w),)),
            pltpu.SemaphoreType.DMA((len(gate_w),)),
            pltpu.SemaphoreType.DMA((len(up_w),)),
            pltpu.SemaphoreType.DMA((14,)),
        ],
        compiler_params=params(),
        cost_estimate=cost(1e6, 1e3),
        name="gate",
    )(at, attended, tokens, gain_table, *out_w, *gate_w, *up_w)

    down_w = [w_down] + on_chips(here, [after(a, mixed) for a in down_arrived], 2)
    down_block = w_down.shape[0] // 4
    down_shape = shape((fsdp, 2, down_block, width), BF16)
    layer_out, d_down, g_ffn_out, down_keep, down_send = pl.pallas_call(
        functools.partial(down_kernel, len(down_w), fsdp),
        out_shape=(
            shape((rows, width), BF16),
            shape((rows, width), BF16),
            shape((1, width), F32),
            down_shape,
            down_shape,
        ),
        in_specs=[SMEM] + [VMEM] * 4 + [ANY] * len(down_w),
        out_specs=(VMEM,) * 5,
        scratch_shapes=[
            pltpu.VMEM((hidden, width), BF16),
            pltpu.VMEM((hidden, rows), BF16),
            pltpu.SemaphoreType.DMA((len(down_w),)),
        ],
        compiler_params=params(),
        cost_estimate=cost(4e9, 2 * weight_bytes),
        name="down",
    )(at, mixed, residual, cotangent, gain_table, *down_w)

    down_sum = Chunk(here, down_keep, down_send)
    gate_shape = shape((fsdp, 2, w_gate.shape[0], hidden // 4), BF16)
    d_gate, d_up, gate_keep, gate_send, up_keep, up_send = pl.pallas_call(
        functools.partial(gate_back_kernel, len(down_w), fsdp),
        out_shape=(
            shape((rows, hidden), BF16),
            shape((rows, hidden), BF16),
            gate_shape,
            gate_shape,
            gate_shape,
            gate_shape,
        ),
        in_specs=[SMEM] + [VMEM] * 4 + [ANY] * len(down_w),
        out_specs=(VMEM,) * 6,
        scratch_shapes=[
            pltpu.VMEM((hidden, width), BF16),
            pltpu.VMEM((width, rows), BF16),
            pltpu.SemaphoreType.DMA((len(down_w),)),
        ],
        compiler_params=params(),
        cost_estimate=cost(6e9, 3 * weight_bytes),
        name="gate_back",
    )(at, d_down, gelu_out, gate_slope, ffn_in, *down_w)
    gate_sum = Chunk(here, gate_keep, gate_send)
    up_sum = Chunk(here, up_keep, up_send)
    down_sum.over_fsdp(d_gate)
    d_gate = after(d_gate, down_sum.other)
    qkv_cols = query_cols + 2 * dim
    last_wide = qkv_cols // 4
    shard_rows = w_query.shape[0]
    last_shape = shape((fsdp, 2, shard_rows + GAIN_ROWS, last_wide), BF16)
    out_block = w_out.shape[0] // 4
    out_shape = shape((fsdp, 2, out_block * width // (hidden // 4), hidden // 4), BF16)
    d_residual, g_ffn, g_attn, d_att, out_keep, out_send = pl.pallas_call(
        functools.partial(middle_kernel, len(out_w), len(gate_w), len(up_w), fsdp, heads),
        out_shape=(
            shape((rows, width), F32),
            shape((1, width), F32),
            shape((1, width), F32),
            shape((heads * rows, dim), BF16),
            out_shape,
            out_shape,
        ),
        in_specs=[SMEM] + [VMEM] * 7 + [ANY] * (len(out_w) + len(gate_w) + len(up_w)),
        out_specs=(VMEM,) * 6,
        scratch_shapes=[
            pltpu.VMEM((query_cols, width), BF16),
            pltpu.VMEM((width, hidden), BF16),
            pltpu.VMEM((width, hidden), BF16),
            pltpu.VMEM((query_cols, rows), BF16),
            pltpu.SemaphoreType.DMA((len(out_w),)),
            pltpu.SemaphoreType.DMA((len(gate_w),)),
            pltpu.SemaphoreType.DMA((len(up_w),)),
        ],
        compiler_params=params(),
        cost_estimate=cost(6e9, 4 * weight_bytes),
        name="middle",
    )(at, d_gate, d_up, residual, projected, cotangent, gain_table, attended, *out_w, *gate_w, *up_w)

    out_sum = Chunk(here, out_keep, out_send)
    gate_sum.over_fsdp(g_ffn)
    up_sum.over_fsdp(g_ffn)
    down_sum.over_mid(g_ffn)
    d_q, d_k, d_v = pl.pallas_call(
        functools.partial(attend_back_kernel, halo, heads),
        out_shape=(shape((rows, query_cols), F32), shape((every, dim), F32), shape((every, dim), F32)),
        in_specs=[VMEM] * 5,
        out_specs=(VMEM,) * 3,
        scratch_shapes=[pltpu.VMEM((heads * QBLOCK, span), BF16)],
        compiler_params=params(),
        cost_estimate=cost(6e9, 3 * weight_bytes),
        name="attend_back",
    )(after(d_att, gate_sum.other, up_sum.other, *down_sum.arrived), q_st, keys, values, probs)
    out_sum.over_fsdp(d_k)
    down_sum.outer_sums(d_k)
    d_q = after(d_q, out_sum.other, down_sum.across)
    grad_tokens, d_halo, last_keep, last_send = pl.pallas_call(
        functools.partial(last_kernel, len(qkv_w), n_tok, fsdp, heads),
        out_shape=(
            shape((rows, width), F32),
            shape((halo, width), BF16),
            last_shape,
            last_shape,
        ),
        in_specs=[SMEM] + [VMEM] * (13 + n_tok) + [ANY] * len(qkv_w),
        out_specs=(VMEM,) * 4,
        scratch_shapes=[
            pltpu.VMEM((width, qkv_cols), BF16),
            pltpu.VMEM((width, every), BF16),
            pltpu.VMEM((every, qkv_cols), BF16),
            pltpu.VMEM((GAIN_ROWS, last_wide), F32),
            pltpu.SemaphoreType.DMA((len(qkv_w),)),
        ],
        compiler_params=params(),
        cost_estimate=cost(15e9, 4 * weight_bytes),
        name="last",
    )(
        at, d_residual, d_q, d_k, d_v,
        q_raw, k_raw, cosine, sine, gain_table, normed, g_ffn, g_attn, g_ffn_out, *toks, *qkv_w,
    )

    last_sum = Chunk(here, last_keep, last_send)
    down_sum.outer_sums(last_keep)
    gate_sum.over_mid(last_keep, *up_sum.arrived)
    (last_sum.other,), (gate_sum.across,), down_sum.shares, out_sum.arrived = together(
        (last_sum.other,), (gate_sum.across,), down_sum.shares, out_sum.arrived
    )
    last_sum.over_fsdp()
    up_sum.join(out_sum)
    gate_sum.outer_sums()
    down_sum.outer_gather()
    last_sum.arrived, (up_sum.across,), gate_sum.shares, down_sum.gathered = together(
        last_sum.arrived, (up_sum.across,), gate_sum.shares, down_sum.gathered
    )
    last_sum.over_mid()
    up_sum.outer_sums()
    gate_sum.outer_gather()
    down_sum.mid_gather()
    (last_sum.across,), up_sum.shares, gate_sum.gathered, down_last = together(
        (last_sum.across,), up_sum.shares, gate_sum.gathered, down_sum.blocks[0]
    )
    down_sum.blocks[0] = list(down_last)
    last_sum.outer_sums()
    up_sum.outer_gather()
    gate_sum.mid_gather()
    last_sum.shares, up_sum.gathered, gate_last = together(last_sum.shares, up_sum.gathered, gate_sum.blocks[0])
    gate_sum.blocks[0] = list(gate_last)
    last_sum.outer_gather()
    up_sum.mid_gather()
    last_sum.mid_gather(up_sum.blocks[0][1])
    d_halo = after(d_halo, up_sum.blocks[0][1])
    halos = [linear_shift(d_halo[halo - by * rows :][:rows], -by) for by in range(1, hops + 1)]
    down_blocks, gate_blocks = by_place(here, down_sum.blocks), by_place(here, gate_sum.blocks)
    both_blocks, last_blocks = by_place(here, up_sum.blocks), by_place(here, last_sum.blocks)
    total_gains = last_sum.blocks[0][0][shard_rows:, :LANES].astype(F32)

    for came in halos:
        grad_tokens = grad_tokens + came.astype(F32)

    total_down = jnp.concatenate(down_blocks, axis=0).astype(F32)
    total_gate = jnp.concatenate(gate_blocks, axis=1).astype(F32)
    total_up = jnp.concatenate([b[:shard_rows] for b in both_blocks], axis=1).astype(F32)
    last_blocks = [b[:shard_rows] for b in last_blocks]
    total_qkv = [last_columns(last_blocks, 0, query_cols)]
    total_qkv += [last_columns(last_blocks, query_cols + i * dim, dim) for i in range(2)]
    wide = hidden // 4
    parts = wide // LANES
    total_out = []
    for block in both_blocks:
        below = block[shard_rows + out_block :].reshape(out_block // parts, parts, LANES)
        below = below.transpose(1, 0, 2).reshape(out_block, LANES)
        total_out.append(jnp.concatenate([block[shard_rows : shard_rows + out_block], below], axis=1))
    total_out = jnp.concatenate(total_out, axis=0).astype(F32)
    g, at_row = [], 0
    for gain in gains:
        deep = fsdp * gain.shape[0] // total_gains.shape[1]
        total = total_gains[at_row : at_row + deep].reshape(fsdp, gain.shape[0])
        g.append(pick(total, here.fsdp_at))
        at_row += deep
    return (
        layer_out, grad_tokens, g[0],
        *total_qkv,
        g[1], g[2], total_out, g[3], g[4], total_gate, total_up, total_down, g[5],
    )


def solution(mesh):
    tok = P(("seq", "fsdp"), None)
    mat = P("fsdp", None)
    vec = P("fsdp")
    return jax.shard_map(
        on_device,
        mesh=mesh,
        in_specs=(tok, P(("seq", "fsdp")), tok, vec, mat, mat, mat, vec, vec, mat, vec, vec, mat, mat, mat, vec),
        out_specs=(tok, tok, vec, mat, mat, mat, vec, vec, mat, vec, vec, mat, mat, mat, vec),
        check_vma=False,
    )
```

profile of v0, /device:TPU:1, one launch (start us, length us, event | category | flops | bytes accessed | tf_op | source)
XLA Modules:
  0.0 247.2 jit_solution(3312662910541493341)
XLA Ops:
  4.5 2.1 collective-permute-start.2
  6.6 3.9 %collective-permute-start = (bf16[256,640]{1,0:T(8,128)(2,1)S(1)}, bf16[256,640]{1,0:T(8,128)(2,1)}, u32[]{:S(2)}, u32[]{:S(2)}) collective-permute-start(bf16[256,640]{1,0:T(8,128)(2,1)S(1)} %copy-done.22), channel_id=1, source_target_pairs={{0,2},{1,3},{2,4},{3,5},{4,6},{5,7},{6,8},{7,9},{8,10},{9,11},{10,... | collective-permute-start | bytes 983048 | tf_op jit(solution)/shard_map/ppermute | solution.py:72
  10.6 2.1 collective-permute-start.1
  16.2 2.5 %multiply_sine_fusion = (f32[768,128]{1,0:T(8,128)}, f32[768,128]{1,0:T(8,128)}) fusion(f32[128]{0:T(128)S(1)} %negate_power_fusion, f32[768]{0:T(1024)S(1)} %add_convert_fusion.10), kind=kLoop, calls=%fused_computation.29 | loop fusion | flops 98304 | bytes 790016 | tf_op jit(solution)/shard_map/sin | solution.py:675
  20.1 1.7 collective-permute-start.3
  22.3 3.2 %collective-permute-done.5.refs_12_.refs_21_ = bf16[320,384]{1,0:T(8,128)(2,1)S(1)} collective-permute-done((bf16[320,384]{1,0:T(8,128)(2,1)}, bf16[320,384]{1,0:T(8,128)(2,1)S(1)}, u32[]{:S(2)}, u32[]{:S(2)}) %collective-permute-start.5) | collective-permute-done | bytes 245792 | tf_op jit(solution)/shard_map/ppermute | solution.py:61
  25.5 1.9 collective-permute-start.7
  29.8 2.0 collective-permute-start.13
  32.8 9.0 %attend.1 = (bf16[768,640]{1,0:T(8,128)(2,1)}, f32[256,1024]{1,0:T(8,128)}, f32[768,256]{1,0:T(8,128)}, bf16[1024,256]{1,0:T(8,128)(2,1)}, bf16[768,256]{1,0:T(8...) custom-call(s32[3]{0:T(128)} %pad_add_fusion.refs_0_, ...), custom_call_target="tpu_custom_call" | custom-call | flops 80000000000 | bytes 200000000 | tf_op jit(solution)/shard_map/attend/pallas_call | solution.py:679
  41.9 10.0 %collective-permute-done.13.refs_13_.refs_17_ = bf16[320,1024]{1,0:T(8,128)(2,1)S(1)} collective-permute-done((bf16[320,1024]{1,0:T(8,128)(2,1)S(1)}, bf16[320,1024]{1,0:T(8,128)(2,1)S(1)}, u32[]{:S(2)}, u32[]{:S(2)}) %collective-permute-start.13) | collective-permute-done | bytes 655392 | tf_op jit(solution)/shard_map/ppermute | solution.py:67
  57.4 9.3 %gate.1 = (f32[256,640]{1,0:T(8,128)}, f32[256,640]{1,0:T(8,128)}, bf16[256,640]{1,0:T(8,128)(2,1)}, bf16[256,2048]{1,0:T(8,128)(2,1)}, bf16[256,2048]{1,0:T(8,128)(2,1)}, /*index=5*/bf16[256,2048]{1,0:T(8,128)(2,1)}) custom-call(s32[3]{0:T(128)} %pad_add_fusion.refs_0_, bf16[256,1024]{1,0:T(8,128)(2,1)} %get-tuple-element.164.refs_1_.refs_7_, ...), custom_call_target="tpu_custom_call" | custom-call | flops 20000000 | bytes 20000 | tf_op jit(solution)/shard_map/gate/pallas_call | solution.py:705
  66.8 2.4 collective-permute-done.15.refs_6_
  69.9 1.7 collective-permute-done.16.refs_7_
  72.5 6.6 %down.1 = (bf16[256,640]{1,0:T(8,128)(2,1)}, bf16[256,640]{1,0:T(8,128)(2,1)}, f32[1,640]{1,0:T(1,128)}, bf16[2,2,256,640]{3,2,1,0:T(8,128)(2,1)}, bf16[2,2,256,640]{3,2,1,0:T(8,128)(2,1)}) custom-call(s32[3]{0:T(128)} %pad_add_fusion.refs_0_, bf16[256,2048]{1,0:T(8,128)(2,1)} %get-tuple-element.170.refs_1_, f32[256,640]{1,0:T(8,128)} %get-tuple-element.171.refs_2_.refs_3_, ...), custom_call_target="tpu_custom_call" | custom-call | flops 80000000000 | bytes 104857600 | tf_op jit(solution)/shard_map/down/pallas_call | solution.py:739
  79.6 10.4 %gate_back.1 = (bf16[256,2048]{1,0:T(8,128)(2,1)}, bf16[256,2048]{1,0:T(8,128)(2,1)}, bf16[2,2,320,512]{3,2,1,0:T(8,128)(2,1)}, bf16[2,2,320,512]{3,2,1,0:T(8,12...) custom-call(s32[3]{0:T(128)} %pad_add_fusion.refs_0_, ...), custom_call_target="tpu_custom_call" | custom-call | flops 120000004096 | bytes 157286400 | tf_op jit(solution)/shard_map/gate_back/pallas_call | solution.py:762
  92.3 10.7 %middle.1 = (f32[256,640]{1,0:T(8,128)}, f32[1,640]{1,0:T(1,128)}, f32[1,640]{1,0:T(1,128)}, bf16[1024,256]{1,0:T(8,128)(2,1)}, bf16[2,2,160,512]{3,2,1,0:T(8,128)(2,1)}, /*index=5*/bf16[2,2,160,512]{3,2,1,0:T(8,128)(2,1)}) custom-call(s32[3]{0:T(128)} %pad_add_fusion.refs_0_, bf16[256,2048]{1,0:T(8,128)(2,1)} %get-tuple-element.181.refs_1_, ...), custom_call_target="tpu_custom_call" | custom-call | flops 120000004096 | bytes 209715200 | tf_op jit(solution)/shard_map/middle/pallas_call | solution.py:793
  109.6 6.4 %attend_back.1 = (f32[256,1024]{1,0:T(8,128)}, f32[768,256]{1,0:T(8,128)}, f32[768,256]{1,0:T(8,128)}) custom-call(bf16[1024,256]{1,0:T(8,128)(2,1)} %get-tuple-element.192.d_att, bf16[1024,256]{1,0:T(8,128)(2,1)} %get-tuple-element.193.q_st, bf16[768,256]{1,0:T(8,128)(2,1)} %get-tuple-element.194.keys, bf16[768,256]{1,0:T(8,128)(2,1)} %get-tuple-element.195.values, ...), custom_call_target="tpu_custom_call" | custom-call | flops 120000004096 | bytes 157286400 | tf_op jit(solution)/shard_map/attend_back/pallas_call | solution.py:823
  116.9 11.7 %last.1 = (f32[256,640]{1,0:T(8,128)}, bf16[512,640]{1,0:T(8,128)(2,1)}, bf16[2,2,352,384]{3,2,1,0:T(8,128)(2,1)}, bf16[2,2,352,384]{3,2,1,0:T(8,128)(2,1)}) custom-call(s32[3]{0:T(128)} %pad_add_fusion.refs_0_, f32[256,640]{1,0:T(8,128)} %get-tuple-element.184.refs_1_, f32[256,1024]{1,0:T(8,128)} %get-tuple-element.201.refs_2_, ...), custom_call_target="tpu_custom_call" | custom-call | flops 299999985664 | bytes 209715200 | tf_op jit(solution)/shard_map/last/pallas_call | solution.py:836
  128.6 2.4 collective-permute-start.23
  132.6 3.7 %collective-permute-done.24 = bf16[2,320,512]{2,1,0:T(8,128)(2,1)} collective-permute-done((bf16[2,320,512]{2,1,0:T(8,128)(2,1)}, bf16[2,320,512]{2,1,0:T(8,128)(2,1)}, u32[]{:S(2)}, u32[]{:S(2)}) %collective-permute-start.24) | collective-permute-done | bytes 655392 | tf_op jit(solution)/shard_map/ppermute | solution.py:67
  140.2 1.3 collective-permute-start.27
  143.3 3.3 %collective-permute-start.29 = (bf16[64,640]{1,0:T(8,128)(2,1)S(1)}, bf16[64,640]{1,0:T(8,128)(2,1)S(1)}, u32[]{:S(2)}, u32[]{:S(2)}) collective-permute-start(bf16[64,640]{1,0:T(8,128)(2,1)S(1)} %get-tuple-element.348), channel_id=1, source_target_pairs={{0,24},{2,26},{4,28},{6,30},{8,0},{10,2},{12,4},{14,6},{16,8},{18,... | collective-permute-start | bytes 245768 | tf_op jit(solution)/shard_map/ppermute | solution.py:64
  148.8 1.4 collective-permute-start.32
  150.9 2.0 collective-permute-start.36
  152.9 1.3 collective-permute-start.37
  159.7 1.5 collective-permute-start.35
  161.9 3.0 %collective-permute-done.34 = bf16[80,512]{1,0:T(8,128)(2,1)S(1)} collective-permute-done((bf16[80,512]{1,0:T(8,128)(2,1)S(1)}, bf16[80,512]{1,0:T(8,128)(2,1)S(1)}, u32[]{:S(2)}, u32[]{:S(2)}) %collective-permute-start.34) | collective-permute-done | bytes 81952 | tf_op jit(solution)/shard_map/ppermute | solution.py:64
  167.0 1.4 collective-permute-start.44
  173.4 1.9 collective-permute-start.42
  175.3 2.6 %collective-permute-done.40 = bf16[120,512]{1,0:T(8,128)(2,1)S(1)} collective-permute-done((bf16[120,512]{1,0:T(8,128)(2,1)S(1)}, bf16[120,512]{1,0:T(8,128)(2,1)S(1)}, u32[]{:S(2)}, u32[]{:S(2)}) %collective-permute-start.40) | collective-permute-done | bytes 122912 | tf_op jit(solution)/shard_map/ppermute | solution.py:64
  177.9 4.3 %collective-permute-done.41 = bf16[120,512]{1,0:T(8,128)(2,1)S(1)} collective-permute-done((bf16[120,512]{1,0:T(8,128)(2,1)S(1)}, bf16[120,512]{1,0:T(8,128)(2,1)S(1)}, u32[]{:S(2)}, u32[]{:S(2)}) %collective-permute-start.41) | collective-permute-done | bytes 122912 | tf_op jit(solution)/shard_map/ppermute | solution.py:64
  183.5 3.5 %collective-permute-start.47 = (bf16[88,384]{1,0:T(8,128)(2,1)S(1)}, bf16[88,384]{1,0:T(8,128)(2,1)S(1)}, u32[]{:S(2)}, u32[]{:S(2)}) collective-permute-start(bf16[88,384]{1,0:T(8,128)(2,1)S(1)} %get-tuple-element.358), channel_id=1, source_target_pairs={{0,8},{2,10},{4,12},{6,14},{8,16},{10,18},{12,20},{14,22},{16,24},... | collective-permute-start | bytes 202760 | tf_op jit(solution)/shard_map/ppermute | solution.py:64
  187.2 2.3 collective-permute-start.51
  189.5 2.8 %collective-permute-start.52 = (bf16[120,512]{1,0:T(8,128)(2,1)S(1)}, bf16[120,512]{1,0:T(8,128)(2,1)S(1)}, u32[]{:S(2)}, u32[]{:S(2)}) collective-permute-start(bf16[120,512]{1,0:T(8,128)(2,1)S(1)} %add_convert_fusion.6), channel_id=1, source_target_pairs={{0,24},{2,26},{4,28},{6,30},{8,0},{10,2},{12,4},{14,6},{16,8},{18,... | collective-permute-start | bytes 368648 | tf_op jit(solution)/shard_map/ppermute | solution.py:64
  192.4 2.4 collective-permute-done.48
  194.8 3.5 %collective-permute-done.49 = bf16[88,384]{1,0:T(8,128)(2,1)S(1)} collective-permute-done((bf16[88,384]{1,0:T(8,128)(2,1)S(1)}, bf16[88,384]{1,0:T(8,128)(2,1)S(1)}, u32[]{:S(2)}, u32[]{:S(2)}) %collective-permute-start.49) | collective-permute-done | bytes 67616 | tf_op jit(solution)/shard_map/ppermute | solution.py:64
  198.3 9.2 %collective-permute-start.67 = (bf16[256,640]{1,0:T(8,128)(2,1)S(1)}, bf16[256,640]{1,0:T(8,128)(2,1)S(1)}, u32[]{:S(2)}, u32[]{:S(2)}) collective-permute-start(bf16[256,640]{1,0:T(8,128)(2,1)S(1)} %bitcast.165), channel_id=1, source_target_pairs={{0,2},{2,0},{4,6},{6,4},{8,10},{10,8},{12,14},{14,12},{16,18},{18,... | collective-permute-start | bytes 983048 | tf_op jit(solution)/shard_map/ppermute | solution.py:58
  209.4 1.5 collective-permute-start.57
  211.5 1.7 maximum_convert_fusion.2
  213.1 1.8 collective-permute-start.58
  215.6 1.8 maximum_convert_fusion
  217.4 2.2 collective-permute-done.58
  223.4 4.5 %collective-permute-start.55 = (bf16[256,640]{1,0:T(8,128)(2,1)}, bf16[256,640]{1,0:T(8,128)(2,1)S(1)}, u32[]{:S(2)}, u32[]{:S(2)}) collective-permute-start(bf16[256,640]{1,0:T(8,128)(2,1)} %get-tuple-element.326), channel_id=1, source_target_pairs={{1,0},{2,1},{3,2},{4,3},{5,4},{6,5},{7,6},{8,7},{9,8},{10,9},{11,1... | collective-permute-start | bytes 983048 | tf_op jit(solution)/shard_map/ppermute | solution.py:72
  227.9 1.9 collective-permute-start.56
  230.5 1.3 reshape.224
  231.8 1.3 reshape.225
  238.2 1.9 convert_add_fusion.6
  241.9 1.8 maximum_convert_fusion.1
  (292 shorter events, 71.4 us)
Async XLA Ops:
  4.5 14.2 %collective-permute-start.2 = (bf16[320,384]{1,0:T(8,128)(2,1)S(1)}, bf16[320,384]{1,0:T(8,128)(2,1)}, u32[]{:S(2)}, u32[]{:S(2)}) collective-permute-start(bf16[320,384]{1,0:T(8,128)(2,1)S(1)} %maximum_select_fusion), channel_id=1, source_target_pairs={{0,1},{1,0},{2,3},{3,2},{4,5},{5,4},{6,7},{7,6},{8,9},{9,8},{10,11... | collective-permute-start | bytes 737288 | tf_op jit(solution)/shard_map/ppermute | solution.py:67
  6.6 21.8 %collective-permute-start = (bf16[256,640]{1,0:T(8,128)(2,1)S(1)}, bf16[256,640]{1,0:T(8,128)(2,1)}, u32[]{:S(2)}, u32[]{:S(2)}) collective-permute-start(bf16[256,640]{1,0:T(8,128)(2,1)S(1)} %copy-done.22), channel_id=1, source_target_pairs={{0,2},{1,3},{2,4},{3,5},{4,6},{5,7},{6,8},{7,9},{8,10},{9,11},{10,... | collective-permute-start | bytes 983048 | tf_op jit(solution)/shard_map/ppermute | solution.py:72
  10.6 17.9 %collective-permute-start.1 = (bf16[256,640]{1,0:T(8,128)(2,1)S(1)}, bf16[256,640]{1,0:T(8,128)(2,1)}, u32[]{:S(2)}, u32[]{:S(2)}) collective-permute-start(bf16[256,640]{1,0:T(8,128)(2,1)S(1)} %copy-done.22), channel_id=1, source_target_pairs={{0,1},{1,2},{2,3},{3,4},{4,5},{5,6},{6,7},{7,8},{8,9},{9,10},{10,1... | collective-permute-start | bytes 983048 | tf_op jit(solution)/shard_map/ppermute | solution.py:72
  12.9 7.2 %collective-permute-start.4 = (bf16[1536]{0:T(1024)(128)(2,1)S(1)}, bf16[1536]{0:T(1024)(128)(2,1)S(1)}, u32[]{:S(2)}, u32[]{:S(2)}) collective-permute-start(bf16[1536]{0:T(1024)(128)(2,1)S(1)} %concatenate.58), channel_id=1, source_target_pairs={{0,1},{1,0},{2,3},{3,2},{4,5},{5,4},{6,7},{7,6},{8,9},{9,8},{10,11... | collective-permute-start | bytes 9224 | tf_op jit(solution)/shard_map/ppermute | solution.py:67
  18.7 6.7 %collective-permute-start.5 = (bf16[320,384]{1,0:T(8,128)(2,1)}, bf16[320,384]{1,0:T(8,128)(2,1)S(1)}, u32[]{:S(2)}, u32[]{:S(2)}) collective-permute-start(bf16[320,384]{1,0:T(8,128)(2,1)} %collective-permute-done.2.refs_11_.refs_20_), channel_id=1, source_target_pairs={{0,4},{2,6},{4,0},{6,2},{8,12},{10,14},{12,8},{14,10},{16,20},{18,... | collective-permute-start | bytes 737288 | tf_op jit(solution)/shard_map/ppermute | solution.py:61
  20.1 8.9 %collective-permute-start.3 = (bf16[320,512]{1,0:T(8,128)(2,1)S(1)}, bf16[320,512]{1,0:T(8,128)(2,1)S(1)}, u32[]{:S(2)}, u32[]{:S(2)}) collective-permute-start(bf16[320,512]{1,0:T(8,128)(2,1)S(1)} %constant_dynamic-slice_fusion.25), channel_id=1, source_target_pairs={{0,1},{1,0},{2,3},{3,2},{4,5},{5,4},{6,7},{7,6},{8,9},{9,8},{10,11... | collective-permute-start | bytes 983048 | tf_op jit(solution)/shard_map/ppermute | solution.py:67
  21.9 10.2 %collective-permute-start.6 = (bf16[320,384]{1,0:T(8,128)(2,1)}, bf16[320,384]{1,0:T(8,128)(2,1)S(1)}, u32[]{:S(2)}, u32[]{:S(2)}) collective-permute-start(bf16[320,384]{1,0:T(8,128)(2,1)} %collective-permute-done.2.refs_11_.refs_20_), channel_id=1, source_target_pairs={{0,2},{2,0},{4,6},{6,4},{8,10},{10,8},{12,14},{14,12},{16,18},{18,... | collective-permute-start | bytes 737288 | tf_op jit(solution)/shard_map/ppermute | solution.py:58
  25.5 6.6 %collective-permute-start.7 = (bf16[320,384]{1,0:T(8,128)(2,1)S(1)}, bf16[320,384]{1,0:T(8,128)(2,1)S(1)}, u32[]{:S(2)}, u32[]{:S(2)}) collective-permute-start(bf16[320,384]{1,0:T(8,128)(2,1)S(1)} %collective-permute-done.5.refs_12_.refs_21_), channel_id=1, source_target_pairs={{0,2},{2,0},{4,6},{6,4},{8,10},{10,8},{12,14},{14,12},{16,18},{18,... | collective-permute-start | bytes 737288 | tf_op jit(solution)/shard_map/ppermute | solution.py:58
  28.5 25.1 %collective-permute-start.8 = (bf16[256,640]{1,0:T(8,128)(2,1)S(1)}, bf16[256,640]{1,0:T(8,128)(2,1)S(1)}, u32[]{:S(2)}, u32[]{:S(2)}) collective-permute-start(bf16[256,640]{1,0:T(8,128)(2,1)S(1)} %constant_dynamic-slice_fusion.24), channel_id=1, source_target_pairs={{0,1},{1,0},{2,3},{3,2},{4,5},{5,4},{6,7},{7,6},{8,9},{9,8},{10,11... | collective-permute-start | bytes 983048 | tf_op jit(solution)/shard_map/ppermute | solution.py:67
  29.8 22.1 %collective-permute-start.13 = (bf16[320,1024]{1,0:T(8,128)(2,1)S(1)}, bf16[320,1024]{1,0:T(8,128)(2,1)S(1)}, u32[]{:S(2)}, u32[]{:S(2)}) collective-permute-start(bf16[320,1024]{1,0:T(8,128)(2,1)S(1)} %constant_dynamic-slice_fusion.23), channel_id=1, source_target_pairs={{0,1},{1,0},{2,3},{3,2},{4,5},{5,4},{6,7},{7,6},{8,9},{9,8},{10,11... | collective-permute-start | bytes 1966088 | tf_op jit(solution)/shard_map/ppermute | solution.py:67
  31.8 22.0 %collective-permute-start.10 = (bf16[320,512]{1,0:T(8,128)(2,1)S(1)}, bf16[320,512]{1,0:T(8,128)(2,1)S(1)}, u32[]{:S(2)}, u32[]{:S(2)}) collective-permute-start(bf16[320,512]{1,0:T(8,128)(2,1)S(1)} %collective-permute-done.3.refs_8_.refs_12_), channel_id=1, source_target_pairs={{0,4},{2,6},{4,0},{6,2},{8,12},{10,14},{12,8},{14,10},{16,20},{18,... | collective-permute-start | bytes 983048 | tf_op jit(solution)/shard_map/ppermute | solution.py:61
  52.7 16.4 %collective-permute-start.15 = (bf16[512,640]{1,0:T(8,128)(2,1)S(1)}, bf16[512,640]{1,0:T(8,128)(2,1)S(1)}, u32[]{:S(2)}, u32[]{:S(2)}) collective-permute-start(bf16[512,640]{1,0:T(8,128)(2,1)S(1)} %constant_dynamic-slice_fusion.22), channel_id=1, source_target_pairs={{0,1},{1,0},{2,3},{3,2},{4,5},{5,4},{6,7},{7,6},{8,9},{9,8},{10,11... | collective-permute-start | bytes 1966088 | tf_op jit(solution)/shard_map/ppermute | solution.py:67
  79.1 11.4 %collective-permute-start.17 = (bf16[2,2,256,640]{3,2,1,0:T(8,128)(2,1)}, bf16[2,2,256,640]{3,2,1,0:T(8,128)(2,1)S(1)}, u32[]{:S(2)}, u32[]{:S(2)}) collective-permute-start(bf16[2,2,256,640]{3,2,1,0:T(8,128)(2,1)} %get-tuple-element.180), channel_id=1, source_target_pairs={{0,2},{2,0},{4,6},{6,4},{8,10},{10,8},{12,14},{14,12},{16,18},{18,... | collective-permute-start | bytes 3932168 | tf_op jit(solution)/shard_map/ppermute | solution.py:58
  90.0 15.7 %collective-permute-start.18 = (bf16[2,2,320,512]{3,2,1,0:T(8,128)(2,1)}, bf16[2,2,320,512]{3,2,1,0:T(8,128)(2,1)S(1)}, u32[]{:S(2)}, u32[]{:S(2)}) collective-permute-start(bf16[2,2,320,512]{3,2,1,0:T(8,128)(2,1)} %get-tuple-element.186), channel_id=1, source_target_pairs={{0,2},{2,0},{4,6},{6,4},{8,10},{10,8},{12,14},{14,12},{16,18},{18,... | collective-permute-start | bytes 3932168 | tf_op jit(solution)/shard_map/ppermute | solution.py:58
  90.2 13.3 %collective-permute-start.19 = (bf16[2,2,320,512]{3,2,1,0:T(8,128)(2,1)}, bf16[2,2,320,512]{3,2,1,0:T(8,128)(2,1)S(1)}, u32[]{:S(2)}, u32[]{:S(2)}) collective-permute-start(bf16[2,2,320,512]{3,2,1,0:T(8,128)(2,1)} %get-tuple-element.187), channel_id=1, source_target_pairs={{0,2},{2,0},{4,6},{6,4},{8,10},{10,8},{12,14},{14,12},{16,18},{18,... | collective-permute-start | bytes 3932168 | tf_op jit(solution)/shard_map/ppermute | solution.py:58
  91.8 16.4 %collective-permute-start.20 = (bf16[2,256,640]{2,1,0:T(8,128)(2,1)}, bf16[2,256,640]{2,1,0:T(8,128)(2,1)S(1)}, u32[]{:S(2)}, u32[]{:S(2)}) collective-permute-start(bf16[2,256,640]{2,1,0:T(8,128)(2,1)} %fusion), channel_id=1, source_target_pairs={{0,1},{1,0},{2,3},{3,2},{4,5},{5,4},{6,7},{7,6},{8,9},{9,8},{10,11... | collective-permute-start | bytes 1966088 | tf_op jit(solution)/shard_map/ppermute | solution.py:67
  103.0 13.2 %collective-permute-start.21 = (bf16[2,2,160,512]{3,2,1,0:T(8,128)(2,1)}, bf16[2,2,160,512]{3,2,1,0:T(8,128)(2,1)S(1)}, u32[]{:S(2)}, u32[]{:S(2)}) collective-permute-start(bf16[2,2,160,512]{3,2,1,0:T(8,128)(2,1)} %get-tuple-element.198), channel_id=1, source_target_pairs={{0,2},{2,0},{4,6},{6,4},{8,10},{10,8},{12,14},{14,12},{16,18},{18,... | collective-permute-start | bytes 1966088 | tf_op jit(solution)/shard_map/ppermute | solution.py:58
  104.7 28.0 %collective-permute-start.25 = (bf16[2,320,512]{2,1,0:T(8,128)(2,1)}, bf16[2,320,512]{2,1,0:T(8,128)(2,1)}, u32[]{:S(2)}, u32[]{:S(2)}) collective-permute-start(bf16[2,320,512]{2,1,0:T(8,128)(2,1)} %fusion.2), channel_id=1, source_target_pairs={{0,1},{1,0},{2,3},{3,2},{4,5},{5,4},{6,7},{7,6},{8,9},{9,8},{10,11... | collective-permute-start | bytes 1966088 | tf_op jit(solution)/shard_map/ppermute | solution.py:67
  106.9 29.5 %collective-permute-start.24 = (bf16[2,320,512]{2,1,0:T(8,128)(2,1)}, bf16[2,320,512]{2,1,0:T(8,128)(2,1)}, u32[]{:S(2)}, u32[]{:S(2)}) collective-permute-start(bf16[2,320,512]{2,1,0:T(8,128)(2,1)} %fusion.1), channel_id=1, source_target_pairs={{0,1},{1,0},{2,3},{3,2},{4,5},{5,4},{6,7},{7,6},{8,9},{9,8},{10,11... | collective-permute-start | bytes 1966088 | tf_op jit(solution)/shard_map/ppermute | solution.py:67
  108.3 7.9 %collective-permute-start.22 = (bf16[256,640]{1,0:T(8,128)(2,1)S(1)}, bf16[256,640]{1,0:T(8,128)(2,1)S(1)}, u32[]{:S(2)}, u32[]{:S(2)}) collective-permute-start(bf16[256,640]{1,0:T(8,128)(2,1)S(1)} %fusion.10), channel_id=1, source_target_pairs={{0,4},{2,6},{4,0},{6,2},{8,12},{10,14},{12,8},{14,10},{16,20},{18,... | collective-permute-start | bytes 983048 | tf_op jit(solution)/shard_map/ppermute | solution.py:61
  128.6 20.0 %collective-permute-start.23 = (bf16[2,2,352,384]{3,2,1,0:T(8,128)(2,1)}, bf16[2,2,352,384]{3,2,1,0:T(8,128)(2,1)S(1)}, u32[]{:S(2)}, u32[]{:S(2)}) collective-permute-start(bf16[2,2,352,384]{3,2,1,0:T(8,128)(2,1)} %get-tuple-element.211), channel_id=1, source_target_pairs={{0,2},{2,0},{4,6},{6,4},{8,10},{10,8},{12,14},{14,12},{16,18},{18,... | collective-permute-start | bytes 3244040 | tf_op jit(solution)/shard_map/ppermute | solution.py:58
  132.1 11.2 %collective-permute-start.30 = (bf16[2,160,512]{2,1,0:T(8,128)(2,1)S(1)}, bf16[2,160,512]{2,1,0:T(8,128)(2,1)S(1)}, u32[]{:S(2)}, u32[]{:S(2)}) collective-permute-start(bf16[2,160,512]{2,1,0:T(8,128)(2,1)S(1)} %fusion.15), channel_id=1, source_target_pairs={{0,1},{1,0},{2,3},{3,2},{4,5},{5,4},{6,7},{7,6},{8,9},{9,8},{10,11... | collective-permute-start | bytes 983048 | tf_op jit(solution)/shard_map/ppermute | solution.py:67
  137.6 11.0 %collective-permute-start.26 = (bf16[320,512]{1,0:T(8,128)(2,1)S(1)}, bf16[320,512]{1,0:T(8,128)(2,1)S(1)}, u32[]{:S(2)}, u32[]{:S(2)}) collective-permute-start(bf16[320,512]{1,0:T(8,128)(2,1)S(1)} %fusion.9), channel_id=1, source_target_pairs={{0,4},{2,6},{4,0},{6,2},{8,12},{10,14},{12,8},{14,10},{16,20},{18,... | collective-permute-start | bytes 983048 | tf_op jit(solution)/shard_map/ppermute | solution.py:61
  140.2 7.7 %collective-permute-start.27 = (bf16[64,640]{1,0:T(8,128)(2,1)S(1)}, bf16[64,640]{1,0:T(8,128)(2,1)S(1)}, u32[]{:S(2)}, u32[]{:S(2)}) collective-permute-start(bf16[64,640]{1,0:T(8,128)(2,1)S(1)} %get-tuple-element.350), channel_id=1, source_target_pairs={{0,8},{2,10},{4,12},{6,14},{8,16},{10,18},{12,20},{14,22},{16,24},... | collective-permute-start | bytes 245768 | tf_op jit(solution)/shard_map/ppermute | solution.py:64
  141.6 7.1 %collective-permute-start.28 = (bf16[64,640]{1,0:T(8,128)(2,1)S(1)}, bf16[64,640]{1,0:T(8,128)(2,1)S(1)}, u32[]{:S(2)}, u32[]{:S(2)}) collective-permute-start(bf16[64,640]{1,0:T(8,128)(2,1)S(1)} %get-tuple-element.349), channel_id=1, source_target_pairs={{0,16},{2,18},{4,20},{6,22},{8,24},{10,26},{12,28},{14,30},{16,0},... | collective-permute-start | bytes 245768 | tf_op jit(solution)/shard_map/ppermute | solution.py:64
  148.8 17.0 %collective-permute-start.32 = (bf16[480,512]{1,0:T(8,128)(2,1)S(1)}, bf16[480,512]{1,0:T(8,128)(2,1)S(1)}, u32[]{:S(2)}, u32[]{:S(2)}) collective-permute-start(bf16[480,512]{1,0:T(8,128)(2,1)S(1)} %pad_maximum_fusion), channel_id=1, source_target_pairs={{0,4},{2,6},{4,0},{6,2},{8,12},{10,14},{12,8},{14,10},{16,20},{18,... | collective-permute-start | bytes 1474568 | tf_op jit(solution)/shard_map/ppermute | solution.py:61
  150.3 15.5 %collective-permute-start.31 = (bf16[2,352,384]{2,1,0:T(8,128)(2,1)S(1)}, bf16[2,352,384]{2,1,0:T(8,128)(2,1)S(1)}, u32[]{:S(2)}, u32[]{:S(2)}) collective-permute-start(bf16[2,352,384]{2,1,0:T(8,128)(2,1)S(1)} %fusion.11), channel_id=1, source_target_pairs={{0,1},{1,0},{2,3},{3,2},{4,5},{5,4},{6,7},{7,6},{8,9},{9,8},{10,11... | collective-permute-start | bytes 1622024 | tf_op jit(solution)/shard_map/ppermute | solution.py:67
  158.1 6.8 %collective-permute-start.34 = (bf16[80,512]{1,0:T(8,128)(2,1)S(1)}, bf16[80,512]{1,0:T(8,128)(2,1)S(1)}, u32[]{:S(2)}, u32[]{:S(2)}) collective-permute-start(bf16[80,512]{1,0:T(8,128)(2,1)S(1)} %get-tuple-element.345), channel_id=1, source_target_pairs={{0,16},{2,18},{4,20},{6,22},{8,24},{10,26},{12,28},{14,30},{16,0},... | collective-permute-start | bytes 245768 | tf_op jit(solution)/shard_map/ppermute | solution.py:64
  159.7 6.1 %collective-permute-start.35 = (bf16[80,512]{1,0:T(8,128)(2,1)S(1)}, bf16[80,512]{1,0:T(8,128)(2,1)S(1)}, u32[]{:S(2)}, u32[]{:S(2)}) collective-permute-start(bf16[80,512]{1,0:T(8,128)(2,1)S(1)} %get-tuple-element.344), channel_id=1, source_target_pairs={{0,24},{2,26},{4,28},{6,30},{8,0},{10,2},{12,4},{14,6},{16,8},{18,... | collective-permute-start | bytes 245768 | tf_op jit(solution)/shard_map/ppermute | solution.py:64
  169.3 12.9 %collective-permute-start.46 = (bf16[256,640]{1,0:T(8,128)(2,1)S(1)}, bf16[256,640]{1,0:T(8,128)(2,1)S(1)}, u32[]{:S(2)}, u32[]{:S(2)}) collective-permute-start(bf16[256,640]{1,0:T(8,128)(2,1)S(1)} %bitcast.164), channel_id=1, source_target_pairs={{0,4},{2,6},{4,0},{6,2},{8,12},{10,14},{12,8},{14,10},{16,20},{18,... | collective-permute-start | bytes 983048 | tf_op jit(solution)/shard_map/ppermute | solution.py:61
  170.6 11.5 %collective-permute-start.39 = (bf16[352,384]{1,0:T(8,128)(2,1)S(1)}, bf16[352,384]{1,0:T(8,128)(2,1)S(1)}, u32[]{:S(2)}, u32[]{:S(2)}) collective-permute-start(bf16[352,384]{1,0:T(8,128)(2,1)S(1)} %fusion.12), channel_id=1, source_target_pairs={{0,4},{2,6},{4,0},{6,2},{8,12},{10,14},{12,8},{14,10},{16,20},{18,... | collective-permute-start | bytes 811016 | tf_op jit(solution)/shard_map/ppermute | solution.py:61
  171.2 6.7 %collective-permute-start.40 = (bf16[120,512]{1,0:T(8,128)(2,1)S(1)}, bf16[120,512]{1,0:T(8,128)(2,1)S(1)}, u32[]{:S(2)}, u32[]{:S(2)}) collective-permute-start(bf16[120,512]{1,0:T(8,128)(2,1)S(1)} %get-tuple-element.334), channel_id=1, source_target_pairs={{0,8},{2,10},{4,12},{6,14},{8,16},{10,18},{12,20},{14,22},{16,24},... | collective-permute-start | bytes 368648 | tf_op jit(solution)/shard_map/ppermute | solution.py:64
  173.0 9.2 %collective-permute-start.41 = (bf16[120,512]{1,0:T(8,128)(2,1)S(1)}, bf16[120,512]{1,0:T(8,128)(2,1)S(1)}, u32[]{:S(2)}, u32[]{:S(2)}) collective-permute-start(bf16[120,512]{1,0:T(8,128)(2,1)S(1)} %get-tuple-element.333), channel_id=1, source_target_pairs={{0,16},{2,18},{4,20},{6,22},{8,24},{10,26},{12,28},{14,30},{16,0},... | collective-permute-start | bytes 368648 | tf_op jit(solution)/shard_map/ppermute | solution.py:64
  173.4 8.8 %collective-permute-start.42 = (bf16[120,512]{1,0:T(8,128)(2,1)S(1)}, bf16[120,512]{1,0:T(8,128)(2,1)S(1)}, u32[]{:S(2)}, u32[]{:S(2)}) collective-permute-start(bf16[120,512]{1,0:T(8,128)(2,1)S(1)} %get-tuple-element.332), channel_id=1, source_target_pairs={{0,24},{2,26},{4,28},{6,30},{8,0},{10,2},{12,4},{14,6},{16,8},{18,... | collective-permute-start | bytes 368648 | tf_op jit(solution)/shard_map/ppermute | solution.py:64
  182.3 25.7 %collective-permute-start.53 = (bf16[320,512]{1,0:T(8,128)(2,1)S(1)}, bf16[320,512]{1,0:T(8,128)(2,1)S(1)}, u32[]{:S(2)}, u32[]{:S(2)}) collective-permute-start(bf16[320,512]{1,0:T(8,128)(2,1)S(1)} %bitcast.167), channel_id=1, source_target_pairs={{0,4},{2,6},{4,0},{6,2},{8,12},{10,14},{12,8},{14,10},{16,20},{18,... | collective-permute-start | bytes 983048 | tf_op jit(solution)/shard_map/ppermute | solution.py:61
  187.0 7.8 %collective-permute-start.48 = (bf16[88,384]{1,0:T(8,128)(2,1)S(1)}, bf16[88,384]{1,0:T(8,128)(2,1)S(1)}, u32[]{:S(2)}, u32[]{:S(2)}) collective-permute-start(bf16[88,384]{1,0:T(8,128)(2,1)S(1)} %get-tuple-element.357), channel_id=1, source_target_pairs={{0,16},{2,18},{4,20},{6,22},{8,24},{10,26},{12,28},{14,30},{16,0},... | collective-permute-start | bytes 202760 | tf_op jit(solution)/shard_map/ppermute | solution.py:64
  187.1 20.5 %collective-permute-start.50 = (bf16[120,512]{1,0:T(8,128)(2,1)S(1)}, bf16[120,512]{1,0:T(8,128)(2,1)S(1)}, u32[]{:S(2)}, u32[]{:S(2)}) collective-permute-start(bf16[120,512]{1,0:T(8,128)(2,1)S(1)} %add_convert_fusion.6), channel_id=1, source_target_pairs={{0,8},{2,10},{4,12},{6,14},{8,16},{10,18},{12,20},{14,22},{16,24},... | collective-permute-start | bytes 368648 | tf_op jit(solution)/shard_map/ppermute | solution.py:64
  187.2 20.3 %collective-permute-start.51 = (bf16[120,512]{1,0:T(8,128)(2,1)S(1)}, bf16[120,512]{1,0:T(8,128)(2,1)S(1)}, u32[]{:S(2)}, u32[]{:S(2)}) collective-permute-start(bf16[120,512]{1,0:T(8,128)(2,1)S(1)} %add_convert_fusion.6), channel_id=1, source_target_pairs={{0,16},{2,18},{4,20},{6,22},{8,24},{10,26},{12,28},{14,30},{16,0},... | collective-permute-start | bytes 368648 | tf_op jit(solution)/shard_map/ppermute | solution.py:64
  189.5 18.5 %collective-permute-start.52 = (bf16[120,512]{1,0:T(8,128)(2,1)S(1)}, bf16[120,512]{1,0:T(8,128)(2,1)S(1)}, u32[]{:S(2)}, u32[]{:S(2)}) collective-permute-start(bf16[120,512]{1,0:T(8,128)(2,1)S(1)} %add_convert_fusion.6), channel_id=1, source_target_pairs={{0,24},{2,26},{4,28},{6,30},{8,0},{10,2},{12,4},{14,6},{16,8},{18,... | collective-permute-start | bytes 368648 | tf_op jit(solution)/shard_map/ppermute | solution.py:64
  198.3 11.1 %collective-permute-start.67 = (bf16[256,640]{1,0:T(8,128)(2,1)S(1)}, bf16[256,640]{1,0:T(8,128)(2,1)S(1)}, u32[]{:S(2)}, u32[]{:S(2)}) collective-permute-start(bf16[256,640]{1,0:T(8,128)(2,1)S(1)} %bitcast.165), channel_id=1, source_target_pairs={{0,2},{2,0},{4,6},{6,4},{8,10},{10,8},{12,14},{14,12},{16,18},{18,... | collective-permute-start | bytes 983048 | tf_op jit(solution)/shard_map/ppermute | solution.py:58
  208.2 12.8 %collective-permute-start.54 = (bf16[480,512]{1,0:T(8,128)(2,1)S(1)}, bf16[480,512]{1,0:T(8,128)(2,1)S(1)}, u32[]{:S(2)}, u32[]{:S(2)}) collective-permute-start(bf16[480,512]{1,0:T(8,128)(2,1)S(1)} %bitcast.161), channel_id=1, source_target_pairs={{0,4},{2,6},{4,0},{6,2},{8,12},{10,14},{12,8},{14,10},{16,20},{18,... | collective-permute-start | bytes 1474568 | tf_op jit(solution)/shard_map/ppermute | solution.py:61
  209.0 31.2 %collective-permute-start.63 = (bf16[480,512]{1,0:T(8,128)(2,1)S(1)}, bf16[480,512]{1,0:T(8,128)(2,1)S(1)}, u32[]{:S(2)}, u32[]{:S(2)}) collective-permute-start(bf16[480,512]{1,0:T(8,128)(2,1)S(1)} %bitcast.162), channel_id=1, source_target_pairs={{0,2},{2,0},{4,6},{6,4},{8,10},{10,8},{12,14},{14,12},{16,18},{18,... | collective-permute-start | bytes 1474568 | tf_op jit(solution)/shard_map/ppermute | solution.py:58
  209.4 8.0 %collective-permute-start.57 = (bf16[88,384]{1,0:T(8,128)(2,1)S(1)}, bf16[88,384]{1,0:T(8,128)(2,1)S(1)}, u32[]{:S(2)}, u32[]{:S(2)}) collective-permute-start(bf16[88,384]{1,0:T(8,128)(2,1)S(1)} %add_convert_fusion.9), channel_id=1, source_target_pairs={{0,8},{2,10},{4,12},{6,14},{8,16},{10,18},{12,20},{14,22},{16,24},... | collective-permute-start | bytes 202760 | tf_op jit(solution)/shard_map/ppermute | solution.py:64
  213.1 6.4 %collective-permute-start.58 = (bf16[88,384]{1,0:T(8,128)(2,1)S(1)}, bf16[88,384]{1,0:T(8,128)(2,1)S(1)}, u32[]{:S(2)}, u32[]{:S(2)}) collective-permute-start(bf16[88,384]{1,0:T(8,128)(2,1)S(1)} %add_convert_fusion.9), channel_id=1, source_target_pairs={{0,16},{2,18},{4,20},{6,22},{8,24},{10,26},{12,28},{14,30},{16,0},... | collective-permute-start | bytes 202760 | tf_op jit(solution)/shard_map/ppermute | solution.py:64
  221.3 16.4 %collective-permute-start.60 = (bf16[352,384]{1,0:T(8,128)(2,1)S(1)}, bf16[352,384]{1,0:T(8,128)(2,1)}, u32[]{:S(2)}, u32[]{:S(2)}) collective-permute-start(bf16[352,384]{1,0:T(8,128)(2,1)S(1)} %bitcast.173), channel_id=1, source_target_pairs={{0,4},{2,6},{4,0},{6,2},{8,12},{10,14},{12,8},{14,10},{16,20},{18,... | collective-permute-start | bytes 811016 | tf_op jit(solution)/shard_map/ppermute | solution.py:61
  223.4 14.8 %collective-permute-start.55 = (bf16[256,640]{1,0:T(8,128)(2,1)}, bf16[256,640]{1,0:T(8,128)(2,1)S(1)}, u32[]{:S(2)}, u32[]{:S(2)}) collective-permute-start(bf16[256,640]{1,0:T(8,128)(2,1)} %get-tuple-element.326), channel_id=1, source_target_pairs={{1,0},{2,1},{3,2},{4,3},{5,4},{6,5},{7,6},{8,7},{9,8},{10,9},{11,1... | collective-permute-start | bytes 983048 | tf_op jit(solution)/shard_map/ppermute | solution.py:72
  227.9 10.4 %collective-permute-start.56 = (bf16[256,640]{1,0:T(8,128)(2,1)S(1)}, bf16[256,640]{1,0:T(8,128)(2,1)}, u32[]{:S(2)}, u32[]{:S(2)}) collective-permute-start(bf16[256,640]{1,0:T(8,128)(2,1)S(1)} %get-tuple-element.327), channel_id=1, source_target_pairs={{2,0},{3,1},{4,2},{5,3},{6,4},{7,5},{8,6},{9,7},{10,8},{11,9},{12,... | collective-permute-start | bytes 983048 | tf_op jit(solution)/shard_map/ppermute | solution.py:72
  229.8 10.4 %collective-permute-start.64 = (bf16[480,512]{1,0:T(8,128)(2,1)S(1)}, bf16[480,512]{1,0:T(8,128)(2,1)S(1)}, u32[]{:S(2)}, u32[]{:S(2)}) collective-permute-start(bf16[480,512]{1,0:T(8,128)(2,1)S(1)} %collective-permute-done.54), channel_id=1, source_target_pairs={{0,2},{2,0},{4,6},{6,4},{8,10},{10,8},{12,14},{14,12},{16,18},{18,... | collective-permute-start | bytes 1474568 | tf_op jit(solution)/shard_map/ppermute | solution.py:58
  (65 other events, 465.9 us)
where the time goes:
time: 249 us; the launch traced here: 247 us
  starting transfers between devices  84.6 us (34%)
  Pallas kernels  64.2 us (26%)
  waiting for transfers between devices  49.1 us (20%)
  other arithmetic  27.7 us (11%)
  local copies, waits for them, and re-layouts  19.4 us (8%)
    ppermute x24, starting transfers between devices, outer_shift(): lax.ppermute(array, 'seq', [(i, (i + 4 * by) % self.seq) for i in range(s...  31.8 us
    ppermute x24, waiting for transfers between devices, outer_shift(): lax.ppermute(array, 'seq', [(i, (i + 4 * by) % self.seq) for i in range(s...  23.6 us
    ppermute x20, starting transfers between devices, core_swap(): return lax.ppermute(array, 'seq', [(i, i ^ 1) for i in range(self.seq)])  19.8 us
    ppermute x11, waiting for transfers between devices, fsdp_shift(): lax.ppermute(array, 'fsdp', [(i, (i + by) % self.fsdp) for i in range(sel...  17.5 us
    ppermute x4, starting transfers between devices, linear_shift(): lax.ppermute(array, ('seq', 'fsdp'), [(i, i + by) for i in range(count) i...  12.5 us
    pallas_call x1, Pallas kernels, on_device(): pl.pallas_call(functools.partial(last_kernel, len(qkv_w), n_tok, fsdp, he...  11.7 us
    ppermute x11, starting transfers between devices, fsdp_shift(): lax.ppermute(array, 'fsdp', [(i, (i + by) % self.fsdp) for i in range(sel...  11 us
    pallas_call x1, Pallas kernels, on_device(): pl.pallas_call(functools.partial(middle_kernel, len(out_w), len(gate_w),...  10.7 us
  transfers between devices with their start and end apart: 69, of which 25 were waited for; matrix products, arithmetic and copies ran while one was open for 14% of the time, Pallas kernels for 23%

commit v1 on v0

--- a/solution.py
+++ b/solution.py
@@ -910,12 +910,12 @@
         below = below.transpose(1, 0, 2).reshape(out_block, LANES)
         total_out.append(jnp.concatenate([block[shard_rows : shard_rows + out_block], below], axis=1))
     total_out = jnp.concatenate(total_out, axis=0).astype(F32)
-    g, at_row = [], 0
+    g, start = [], 0
+    flat = total_gains.reshape(-1)
     for gain in gains:
-        deep = fsdp * gain.shape[0] // total_gains.shape[1]
-        total = total_gains[at_row : at_row + deep].reshape(fsdp, gain.shape[0])
-        g.append(pick(total, here.fsdp_at))
-        at_row += deep
+        size = gain.shape[0]
+        g.append(lax.dynamic_slice_in_dim(flat, start + here.fsdp_at * size, size, 0, allow_negative_indices=False))
+        start += fsdp * size
     return (
         layer_out, grad_tokens, g[0],
         *total_qkv,

time: 249 us -> 245 us (0.984)
  local copies, waits for them, and re-layouts: 19.4 us -> 11.6 us
  starting transfers between devices: 84.6 us -> 91.1 us
    ppermute x20, starting transfers between devices: 19.8 us -> 26.8 us  [core_swap(): return lax.ppermute(array, 'seq', [(i, i ^ 1) for i in range(self.seq)])]
    reshape x4 -> x0, local copies, waits for them, and re-layouts: 3.41 us -> none  [on_device(): total = total_gains[at_row:at_row + deep].reshape(fsdp, gain.shape[0])]
    dynamic_slice x6 -> x4, local copies, waits for them, and re-layouts: 2.77 us -> 0.18 us  [pick(): lax.dynamic_index_in_dim(array, at, 0, keepdims=False, allow_negative_ind...]
  transfers between devices with their start and end apart: 69 -> 69, of which waited for: 25 -> 27; matrix products, arithmetic and copies ran while one was open for 14% -> 11% of each run, Pallas kernels for 23% -> 24%
where the time goes in v1:
time: 245 us; the launch traced here: 244 us
  starting transfers between devices  91.1 us (37%)
  Pallas kernels  64.2 us (26%)
  waiting for transfers between devices  49.6 us (20%)
  other arithmetic  25.7 us (10%)
  local copies, waits for them, and re-layouts  11.6 us (5%)
    ppermute x24, starting transfers between devices, outer_shift(): lax.ppermute(array, 'seq', [(i, (i + 4 * by) % self.seq) for i in range(s...  33.3 us
    ppermute x20, starting transfers between devices, core_swap(): return lax.ppermute(array, 'seq', [(i, i ^ 1) for i in range(self.seq)])  26.8 us
    ppermute x24, waiting for transfers between devices, outer_shift(): lax.ppermute(array, 'seq', [(i, (i + 4 * by) % self.seq) for i in range(s...  21.3 us
    ppermute x11, waiting for transfers between devices, fsdp_shift(): lax.ppermute(array, 'fsdp', [(i, (i + by) % self.fsdp) for i in range(sel...  17.5 us
    pallas_call x1, Pallas kernels, on_device(): pl.pallas_call(functools.partial(last_kernel, len(qkv_w), n_tok, fsdp, he...  11.7 us
    ppermute x4, starting transfers between devices, linear_shift(): lax.ppermute(array, ('seq', 'fsdp'), [(i, i + by) for i in range(count) i...  11.5 us
    ppermute x11, starting transfers between devices, fsdp_shift(): lax.ppermute(array, 'fsdp', [(i, (i + by) % self.fsdp) for i in range(sel...  11 us
    pallas_call x1, Pallas kernels, on_device(): pl.pallas_call(functools.partial(middle_kernel, len(out_w), len(gate_w),...  10.7 us
  transfers between devices with their start and end apart: 69, of which 27 were waited for; matrix products, arithmetic and copies ran while one was open for 11% of the time, Pallas kernels for 24%

profile of v1, /device:TPU:1, one launch (start us, length us, event | category | flops | bytes accessed | tf_op | source)
XLA Modules:
  0.0 244.4 jit_solution(7985371744716852800)
XLA Ops:
  4.5 2.1 collective-permute-start.2
  6.7 3.9 %collective-permute-start = (bf16[256,640]{1,0:T(8,128)(2,1)S(1)}, bf16[256,640]{1,0:T(8,128)(2,1)}, u32[]{:S(2)}, u32[]{:S(2)}) collective-permute-start(bf16[256,640]{1,0:T(8,128)(2,1)S(1)} %copy-done.22), channel_id=1, source_target_pairs={{0,2},{1,3},{2,4},{3,5},{4,6},{5,7},{6,8},{7,9},{8,10},{9,11},{10,... | collective-permute-start | bytes 983048 | tf_op jit(solution)/shard_map/ppermute | solution.py:72
  10.6 2.1 collective-permute-start.1
  16.2 2.5 %multiply_sine_fusion = (f32[768,128]{1,0:T(8,128)}, f32[768,128]{1,0:T(8,128)}) fusion(f32[128]{0:T(128)S(1)} %negate_power_fusion, f32[768]{0:T(1024)S(1)} %add_convert_fusion.10), kind=kLoop, calls=%fused_computation.29 | loop fusion | flops 98304 | bytes 790016 | tf_op jit(solution)/shard_map/sin | solution.py:675
  20.2 1.7 collective-permute-start.3
  22.3 3.2 %collective-permute-done.5.refs_12_.refs_21_ = bf16[320,384]{1,0:T(8,128)(2,1)S(1)} collective-permute-done((bf16[320,384]{1,0:T(8,128)(2,1)}, bf16[320,384]{1,0:T(8,128)(2,1)S(1)}, u32[]{:S(2)}, u32[]{:S(2)}) %collective-permute-start.5) | collective-permute-done | bytes 245792 | tf_op jit(solution)/shard_map/ppermute | solution.py:61
  25.5 1.9 collective-permute-start.7
  29.8 2.0 collective-permute-start.13
  32.9 9.0 %attend.1 = (bf16[768,640]{1,0:T(8,128)(2,1)}, f32[256,1024]{1,0:T(8,128)}, f32[768,256]{1,0:T(8,128)}, bf16[1024,256]{1,0:T(8,128)(2,1)}, bf16[768,256]{1,0:T(8...) custom-call(s32[3]{0:T(128)} %pad_add_fusion.refs_0_, ...), custom_call_target="tpu_custom_call" | custom-call | flops 80000000000 | bytes 200000000 | tf_op jit(solution)/shard_map/attend/pallas_call | solution.py:679
  41.9 10.0 %collective-permute-done.13.refs_13_.refs_17_ = bf16[320,1024]{1,0:T(8,128)(2,1)S(1)} collective-permute-done((bf16[320,1024]{1,0:T(8,128)(2,1)S(1)}, bf16[320,1024]{1,0:T(8,128)(2,1)S(1)}, u32[]{:S(2)}, u32[]{:S(2)}) %collective-permute-start.13) | collective-permute-done | bytes 655392 | tf_op jit(solution)/shard_map/ppermute | solution.py:67
  57.5 9.3 %gate.1 = (f32[256,640]{1,0:T(8,128)}, f32[256,640]{1,0:T(8,128)}, bf16[256,640]{1,0:T(8,128)(2,1)}, bf16[256,2048]{1,0:T(8,128)(2,1)}, bf16[256,2048]{1,0:T(8,128)(2,1)}, /*index=5*/bf16[256,2048]{1,0:T(8,128)(2,1)}) custom-call(s32[3]{0:T(128)} %pad_add_fusion.refs_0_, bf16[256,1024]{1,0:T(8,128)(2,1)} %get-tuple-element.164.refs_1_.refs_7_, ...), custom_call_target="tpu_custom_call" | custom-call | flops 20000000 | bytes 20000 | tf_op jit(solution)/shard_map/gate/pallas_call | solution.py:705
  66.8 2.4 collective-permute-done.15.refs_6_
  70.0 1.7 collective-permute-done.16.refs_7_
  72.5 6.6 %down.1 = (bf16[256,640]{1,0:T(8,128)(2,1)}, bf16[256,640]{1,0:T(8,128)(2,1)}, f32[1,640]{1,0:T(1,128)}, bf16[2,2,256,640]{3,2,1,0:T(8,128)(2,1)}, bf16[2,2,256,640]{3,2,1,0:T(8,128)(2,1)}) custom-call(s32[3]{0:T(128)} %pad_add_fusion.refs_0_, bf16[256,2048]{1,0:T(8,128)(2,1)} %get-tuple-element.170.refs_1_, f32[256,640]{1,0:T(8,128)} %get-tuple-element.171.refs_2_.refs_3_, ...), custom_call_target="tpu_custom_call" | custom-call | flops 80000000000 | bytes 104857600 | tf_op jit(solution)/shard_map/down/pallas_call | solution.py:739
  79.6 10.4 %gate_back.1 = (bf16[256,2048]{1,0:T(8,128)(2,1)}, bf16[256,2048]{1,0:T(8,128)(2,1)}, bf16[2,2,320,512]{3,2,1,0:T(8,128)(2,1)}, bf16[2,2,320,512]{3,2,1,0:T(8,12...) custom-call(s32[3]{0:T(128)} %pad_add_fusion.refs_0_, ...), custom_call_target="tpu_custom_call" | custom-call | flops 120000004096 | bytes 157286400 | tf_op jit(solution)/shard_map/gate_back/pallas_call | solution.py:762
  92.3 10.7 %middle.1 = (f32[256,640]{1,0:T(8,128)}, f32[1,640]{1,0:T(1,128)}, f32[1,640]{1,0:T(1,128)}, bf16[1024,256]{1,0:T(8,128)(2,1)}, bf16[2,2,160,512]{3,2,1,0:T(8,128)(2,1)}, /*index=5*/bf16[2,2,160,512]{3,2,1,0:T(8,128)(2,1)}) custom-call(s32[3]{0:T(128)} %pad_add_fusion.refs_0_, bf16[256,2048]{1,0:T(8,128)(2,1)} %get-tuple-element.181.refs_1_, ...), custom_call_target="tpu_custom_call" | custom-call | flops 120000004096 | bytes 209715200 | tf_op jit(solution)/shard_map/middle/pallas_call | solution.py:793
  108.4 1.3 collective-permute-start.22
  109.7 6.4 %attend_back.1 = (f32[256,1024]{1,0:T(8,128)}, f32[768,256]{1,0:T(8,128)}, f32[768,256]{1,0:T(8,128)}) custom-call(bf16[1024,256]{1,0:T(8,128)(2,1)} %get-tuple-element.192.d_att, bf16[1024,256]{1,0:T(8,128)(2,1)} %get-tuple-element.193.q_st, bf16[768,256]{1,0:T(8,128)(2,1)} %get-tuple-element.194.keys, bf16[768,256]{1,0:T(8,128)(2,1)} %get-tuple-element.195.values, ...), custom_call_target="tpu_custom_call" | custom-call | flops 120000004096 | bytes 157286400 | tf_op jit(solution)/shard_map/attend_back/pallas_call | solution.py:823
  117.0 11.7 %last.1 = (f32[256,640]{1,0:T(8,128)}, bf16[512,640]{1,0:T(8,128)(2,1)}, bf16[2,2,352,384]{3,2,1,0:T(8,128)(2,1)}, bf16[2,2,352,384]{3,2,1,0:T(8,128)(2,1)}) custom-call(s32[3]{0:T(128)} %pad_add_fusion.refs_0_, f32[256,640]{1,0:T(8,128)} %get-tuple-element.184.refs_1_, f32[256,1024]{1,0:T(8,128)} %get-tuple-element.201.refs_2_, ...), custom_call_target="tpu_custom_call" | custom-call | flops 299999985664 | bytes 209715200 | tf_op jit(solution)/shard_map/last/pallas_call | solution.py:836
  128.7 2.4 collective-permute-start.23
  132.7 3.7 %collective-permute-done.24 = bf16[2,320,512]{2,1,0:T(8,128)(2,1)} collective-permute-done((bf16[2,320,512]{2,1,0:T(8,128)(2,1)}, bf16[2,320,512]{2,1,0:T(8,128)(2,1)}, u32[]{:S(2)}, u32[]{:S(2)}) %collective-permute-start.24) | collective-permute-done | bytes 655392 | tf_op jit(solution)/shard_map/ppermute | solution.py:67
  140.3 1.4 collective-permute-start.27
  143.3 3.3 %collective-permute-start.29 = (bf16[64,640]{1,0:T(8,128)(2,1)S(1)}, bf16[64,640]{1,0:T(8,128)(2,1)S(1)}, u32[]{:S(2)}, u32[]{:S(2)}) collective-permute-start(bf16[64,640]{1,0:T(8,128)(2,1)S(1)} %get-tuple-element.348), channel_id=1, source_target_pairs={{0,24},{2,26},{4,28},{6,30},{8,0},{10,2},{12,4},{14,6},{16,8},{18,... | collective-permute-start | bytes 245768 | tf_op jit(solution)/shard_map/ppermute | solution.py:64
  150.6 2.2 collective-permute-start.36
  152.8 1.5 collective-permute-start.37
  159.6 1.6 collective-permute-start.35
  161.8 2.5 %collective-permute-done.34 = bf16[80,512]{1,0:T(8,128)(2,1)S(1)} collective-permute-done((bf16[80,512]{1,0:T(8,128)(2,1)S(1)}, bf16[80,512]{1,0:T(8,128)(2,1)S(1)}, u32[]{:S(2)}, u32[]{:S(2)}) %collective-permute-start.34) | collective-permute-done | bytes 81952 | tf_op jit(solution)/shard_map/ppermute | solution.py:64
  164.9 2.0 collective-permute-start.43
  166.8 1.5 collective-permute-start.44
  173.1 2.0 collective-permute-start.42
  175.1 2.1 collective-permute-done.40
  177.2 5.1 %collective-permute-done.41 = bf16[120,512]{1,0:T(8,128)(2,1)S(1)} collective-permute-done((bf16[120,512]{1,0:T(8,128)(2,1)S(1)}, bf16[120,512]{1,0:T(8,128)(2,1)S(1)}, u32[]{:S(2)}, u32[]{:S(2)}) %collective-permute-start.41) | collective-permute-done | bytes 122912 | tf_op jit(solution)/shard_map/ppermute | solution.py:64
  183.8 3.5 %collective-permute-start.47 = (bf16[88,384]{1,0:T(8,128)(2,1)S(1)}, bf16[88,384]{1,0:T(8,128)(2,1)S(1)}, u32[]{:S(2)}, u32[]{:S(2)}) collective-permute-start(bf16[88,384]{1,0:T(8,128)(2,1)S(1)} %get-tuple-element.358), channel_id=1, source_target_pairs={{0,8},{2,10},{4,12},{6,14},{8,16},{10,18},{12,20},{14,22},{16,24},... | collective-permute-start | bytes 202760 | tf_op jit(solution)/shard_map/ppermute | solution.py:64
  187.5 2.3 collective-permute-start.51
  189.9 2.3 collective-permute-start.52
  192.2 2.4 collective-permute-done.48
  194.6 3.8 %collective-permute-done.49 = bf16[88,384]{1,0:T(8,128)(2,1)S(1)} collective-permute-done((bf16[88,384]{1,0:T(8,128)(2,1)S(1)}, bf16[88,384]{1,0:T(8,128)(2,1)S(1)}, u32[]{:S(2)}, u32[]{:S(2)}) %collective-permute-start.49) | collective-permute-done | bytes 67616 | tf_op jit(solution)/shard_map/ppermute | solution.py:64
  198.4 10.0 %collective-permute-start.67 = (bf16[256,640]{1,0:T(8,128)(2,1)S(1)}, bf16[256,640]{1,0:T(8,128)(2,1)S(1)}, u32[]{:S(2)}, u32[]{:S(2)}) collective-permute-start(bf16[256,640]{1,0:T(8,128)(2,1)S(1)} %bitcast.166), channel_id=1, source_target_pairs={{0,2},{2,0},{4,6},{6,4},{8,10},{10,8},{12,14},{14,12},{16,18},{18,... | collective-permute-start | bytes 983048 | tf_op jit(solution)/shard_map/ppermute | solution.py:58
  209.6 1.4 collective-permute-start.57
  211.9 1.7 maximum_convert_fusion.2
  213.6 1.8 collective-permute-start.58
  216.4 1.8 maximum_convert_fusion
  218.2 1.5 collective-permute-done.58
  219.7 2.2 collective-permute-done.54
  222.4 3.4 %collective-permute-start.55 = (bf16[256,640]{1,0:T(8,128)(2,1)S(1)}, bf16[256,640]{1,0:T(8,128)(2,1)S(1)}, u32[]{:S(2)}, u32[]{:S(2)}) collective-permute-start(bf16[256,640]{1,0:T(8,128)(2,1)S(1)} %get-tuple-element.326), channel_id=1, source_target_pairs={{1,0},{2,1},{3,2},{4,3},{5,4},{6,5},{7,6},{8,7},{9,8},{10,9},{11,1... | collective-permute-start | bytes 983048 | tf_op jit(solution)/shard_map/ppermute | solution.py:72
  225.9 1.9 collective-permute-start.56
  229.3 6.8 %collective-permute-start.61 = (bf16[352,384]{1,0:T(8,128)(2,1)S(1)}, bf16[352,384]{1,0:T(8,128)(2,1)S(1)}, u32[]{:S(2)}, u32[]{:S(2)}) collective-permute-start(bf16[352,384]{1,0:T(8,128)(2,1)S(1)} %bitcast.175), channel_id=1, source_target_pairs={{0,2},{2,0},{4,6},{6,4},{8,10},{10,8},{12,14},{14,12},{16,18},{18,... | collective-permute-start | bytes 811016 | tf_op jit(solution)/shard_map/ppermute | solution.py:58
  240.1 1.8 maximum_convert_fusion.1
  (285 shorter events, 63.2 us)
Async XLA Ops:
  4.5 14.3 %collective-permute-start.2 = (bf16[320,384]{1,0:T(8,128)(2,1)S(1)}, bf16[320,384]{1,0:T(8,128)(2,1)}, u32[]{:S(2)}, u32[]{:S(2)}) collective-permute-start(bf16[320,384]{1,0:T(8,128)(2,1)S(1)} %maximum_select_fusion), channel_id=1, source_target_pairs={{0,1},{1,0},{2,3},{3,2},{4,5},{5,4},{6,7},{7,6},{8,9},{9,8},{10,11... | collective-permute-start | bytes 737288 | tf_op jit(solution)/shard_map/ppermute | solution.py:67
  6.7 21.9 %collective-permute-start = (bf16[256,640]{1,0:T(8,128)(2,1)S(1)}, bf16[256,640]{1,0:T(8,128)(2,1)}, u32[]{:S(2)}, u32[]{:S(2)}) collective-permute-start(bf16[256,640]{1,0:T(8,128)(2,1)S(1)} %copy-done.22), channel_id=1, source_target_pairs={{0,2},{1,3},{2,4},{3,5},{4,6},{5,7},{6,8},{7,9},{8,10},{9,11},{10,... | collective-permute-start | bytes 983048 | tf_op jit(solution)/shard_map/ppermute | solution.py:72
  10.6 17.9 %collective-permute-start.1 = (bf16[256,640]{1,0:T(8,128)(2,1)S(1)}, bf16[256,640]{1,0:T(8,128)(2,1)}, u32[]{:S(2)}, u32[]{:S(2)}) collective-permute-start(bf16[256,640]{1,0:T(8,128)(2,1)S(1)} %copy-done.22), channel_id=1, source_target_pairs={{0,1},{1,2},{2,3},{3,4},{4,5},{5,6},{6,7},{7,8},{8,9},{9,10},{10,1... | collective-permute-start | bytes 983048 | tf_op jit(solution)/shard_map/ppermute | solution.py:72
  12.9 7.2 %collective-permute-start.4 = (bf16[1536]{0:T(1024)(128)(2,1)S(1)}, bf16[1536]{0:T(1024)(128)(2,1)S(1)}, u32[]{:S(2)}, u32[]{:S(2)}) collective-permute-start(bf16[1536]{0:T(1024)(128)(2,1)S(1)} %concatenate.58), channel_id=1, source_target_pairs={{0,1},{1,0},{2,3},{3,2},{4,5},{5,4},{6,7},{7,6},{8,9},{9,8},{10,11... | collective-permute-start | bytes 9224 | tf_op jit(solution)/shard_map/ppermute | solution.py:67
  18.8 6.7 %collective-permute-start.5 = (bf16[320,384]{1,0:T(8,128)(2,1)}, bf16[320,384]{1,0:T(8,128)(2,1)S(1)}, u32[]{:S(2)}, u32[]{:S(2)}) collective-permute-start(bf16[320,384]{1,0:T(8,128)(2,1)} %collective-permute-done.2.refs_11_.refs_20_), channel_id=1, source_target_pairs={{0,4},{2,6},{4,0},{6,2},{8,12},{10,14},{12,8},{14,10},{16,20},{18,... | collective-permute-start | bytes 737288 | tf_op jit(solution)/shard_map/ppermute | solution.py:61
  20.2 8.9 %collective-permute-start.3 = (bf16[320,512]{1,0:T(8,128)(2,1)S(1)}, bf16[320,512]{1,0:T(8,128)(2,1)S(1)}, u32[]{:S(2)}, u32[]{:S(2)}) collective-permute-start(bf16[320,512]{1,0:T(8,128)(2,1)S(1)} %constant_dynamic-slice_fusion.19), channel_id=1, source_target_pairs={{0,1},{1,0},{2,3},{3,2},{4,5},{5,4},{6,7},{7,6},{8,9},{9,8},{10,11... | collective-permute-start | bytes 983048 | tf_op jit(solution)/shard_map/ppermute | solution.py:67
  21.9 10.2 %collective-permute-start.6 = (bf16[320,384]{1,0:T(8,128)(2,1)}, bf16[320,384]{1,0:T(8,128)(2,1)S(1)}, u32[]{:S(2)}, u32[]{:S(2)}) collective-permute-start(bf16[320,384]{1,0:T(8,128)(2,1)} %collective-permute-done.2.refs_11_.refs_20_), channel_id=1, source_target_pairs={{0,2},{2,0},{4,6},{6,4},{8,10},{10,8},{12,14},{14,12},{16,18},{18,... | collective-permute-start | bytes 737288 | tf_op jit(solution)/shard_map/ppermute | solution.py:58
  25.5 6.6 %collective-permute-start.7 = (bf16[320,384]{1,0:T(8,128)(2,1)S(1)}, bf16[320,384]{1,0:T(8,128)(2,1)S(1)}, u32[]{:S(2)}, u32[]{:S(2)}) collective-permute-start(bf16[320,384]{1,0:T(8,128)(2,1)S(1)} %collective-permute-done.5.refs_12_.refs_21_), channel_id=1, source_target_pairs={{0,2},{2,0},{4,6},{6,4},{8,10},{10,8},{12,14},{14,12},{16,18},{18,... | collective-permute-start | bytes 737288 | tf_op jit(solution)/shard_map/ppermute | solution.py:58
  28.5 25.1 %collective-permute-start.8 = (bf16[256,640]{1,0:T(8,128)(2,1)S(1)}, bf16[256,640]{1,0:T(8,128)(2,1)S(1)}, u32[]{:S(2)}, u32[]{:S(2)}) collective-permute-start(bf16[256,640]{1,0:T(8,128)(2,1)S(1)} %constant_dynamic-slice_fusion.18), channel_id=1, source_target_pairs={{0,1},{1,0},{2,3},{3,2},{4,5},{5,4},{6,7},{7,6},{8,9},{9,8},{10,11... | collective-permute-start | bytes 983048 | tf_op jit(solution)/shard_map/ppermute | solution.py:67
  29.8 22.1 %collective-permute-start.13 = (bf16[320,1024]{1,0:T(8,128)(2,1)S(1)}, bf16[320,1024]{1,0:T(8,128)(2,1)S(1)}, u32[]{:S(2)}, u32[]{:S(2)}) collective-permute-start(bf16[320,1024]{1,0:T(8,128)(2,1)S(1)} %constant_dynamic-slice_fusion.17), channel_id=1, source_target_pairs={{0,1},{1,0},{2,3},{3,2},{4,5},{5,4},{6,7},{7,6},{8,9},{9,8},{10,11... | collective-permute-start | bytes 1966088 | tf_op jit(solution)/shard_map/ppermute | solution.py:67
  31.8 22.0 %collective-permute-start.10 = (bf16[320,512]{1,0:T(8,128)(2,1)S(1)}, bf16[320,512]{1,0:T(8,128)(2,1)S(1)}, u32[]{:S(2)}, u32[]{:S(2)}) collective-permute-start(bf16[320,512]{1,0:T(8,128)(2,1)S(1)} %collective-permute-done.3.refs_8_.refs_12_), channel_id=1, source_target_pairs={{0,4},{2,6},{4,0},{6,2},{8,12},{10,14},{12,8},{14,10},{16,20},{18,... | collective-permute-start | bytes 983048 | tf_op jit(solution)/shard_map/ppermute | solution.py:61
  52.8 16.4 %collective-permute-start.15 = (bf16[512,640]{1,0:T(8,128)(2,1)S(1)}, bf16[512,640]{1,0:T(8,128)(2,1)S(1)}, u32[]{:S(2)}, u32[]{:S(2)}) collective-permute-start(bf16[512,640]{1,0:T(8,128)(2,1)S(1)} %constant_dynamic-slice_fusion.16), channel_id=1, source_target_pairs={{0,1},{1,0},{2,3},{3,2},{4,5},{5,4},{6,7},{7,6},{8,9},{9,8},{10,11... | collective-permute-start | bytes 1966088 | tf_op jit(solution)/shard_map/ppermute | solution.py:67
  79.2 11.4 %collective-permute-start.17 = (bf16[2,2,256,640]{3,2,1,0:T(8,128)(2,1)}, bf16[2,2,256,640]{3,2,1,0:T(8,128)(2,1)S(1)}, u32[]{:S(2)}, u32[]{:S(2)}) collective-permute-start(bf16[2,2,256,640]{3,2,1,0:T(8,128)(2,1)} %get-tuple-element.180), channel_id=1, source_target_pairs={{0,2},{2,0},{4,6},{6,4},{8,10},{10,8},{12,14},{14,12},{16,18},{18,... | collective-permute-start | bytes 3932168 | tf_op jit(solution)/shard_map/ppermute | solution.py:58
  90.0 15.8 %collective-permute-start.18 = (bf16[2,2,320,512]{3,2,1,0:T(8,128)(2,1)}, bf16[2,2,320,512]{3,2,1,0:T(8,128)(2,1)S(1)}, u32[]{:S(2)}, u32[]{:S(2)}) collective-permute-start(bf16[2,2,320,512]{3,2,1,0:T(8,128)(2,1)} %get-tuple-element.186), channel_id=1, source_target_pairs={{0,2},{2,0},{4,6},{6,4},{8,10},{10,8},{12,14},{14,12},{16,18},{18,... | collective-permute-start | bytes 3932168 | tf_op jit(solution)/shard_map/ppermute | solution.py:58
  90.2 13.4 %collective-permute-start.19 = (bf16[2,2,320,512]{3,2,1,0:T(8,128)(2,1)}, bf16[2,2,320,512]{3,2,1,0:T(8,128)(2,1)S(1)}, u32[]{:S(2)}, u32[]{:S(2)}) collective-permute-start(bf16[2,2,320,512]{3,2,1,0:T(8,128)(2,1)} %get-tuple-element.187), channel_id=1, source_target_pairs={{0,2},{2,0},{4,6},{6,4},{8,10},{10,8},{12,14},{14,12},{16,18},{18,... | collective-permute-start | bytes 3932168 | tf_op jit(solution)/shard_map/ppermute | solution.py:58
  91.8 16.4 %collective-permute-start.20 = (bf16[2,256,640]{2,1,0:T(8,128)(2,1)}, bf16[2,256,640]{2,1,0:T(8,128)(2,1)S(1)}, u32[]{:S(2)}, u32[]{:S(2)}) collective-permute-start(bf16[2,256,640]{2,1,0:T(8,128)(2,1)} %fusion), channel_id=1, source_target_pairs={{0,1},{1,0},{2,3},{3,2},{4,5},{5,4},{6,7},{7,6},{8,9},{9,8},{10,11... | collective-permute-start | bytes 1966088 | tf_op jit(solution)/shard_map/ppermute | solution.py:67
  103.1 13.2 %collective-permute-start.21 = (bf16[2,2,160,512]{3,2,1,0:T(8,128)(2,1)}, bf16[2,2,160,512]{3,2,1,0:T(8,128)(2,1)S(1)}, u32[]{:S(2)}, u32[]{:S(2)}) collective-permute-start(bf16[2,2,160,512]{3,2,1,0:T(8,128)(2,1)} %get-tuple-element.198), channel_id=1, source_target_pairs={{0,2},{2,0},{4,6},{6,4},{8,10},{10,8},{12,14},{14,12},{16,18},{18,... | collective-permute-start | bytes 1966088 | tf_op jit(solution)/shard_map/ppermute | solution.py:58
  104.8 27.9 %collective-permute-start.25 = (bf16[2,320,512]{2,1,0:T(8,128)(2,1)}, bf16[2,320,512]{2,1,0:T(8,128)(2,1)}, u32[]{:S(2)}, u32[]{:S(2)}) collective-permute-start(bf16[2,320,512]{2,1,0:T(8,128)(2,1)} %fusion.2), channel_id=1, source_target_pairs={{0,1},{1,0},{2,3},{3,2},{4,5},{5,4},{6,7},{7,6},{8,9},{9,8},{10,11... | collective-permute-start | bytes 1966088 | tf_op jit(solution)/shard_map/ppermute | solution.py:67
  106.9 29.5 %collective-permute-start.24 = (bf16[2,320,512]{2,1,0:T(8,128)(2,1)}, bf16[2,320,512]{2,1,0:T(8,128)(2,1)}, u32[]{:S(2)}, u32[]{:S(2)}) collective-permute-start(bf16[2,320,512]{2,1,0:T(8,128)(2,1)} %fusion.1), channel_id=1, source_target_pairs={{0,1},{1,0},{2,3},{3,2},{4,5},{5,4},{6,7},{7,6},{8,9},{9,8},{10,11... | collective-permute-start | bytes 1966088 | tf_op jit(solution)/shard_map/ppermute | solution.py:67
  108.4 7.9 %collective-permute-start.22 = (bf16[256,640]{1,0:T(8,128)(2,1)S(1)}, bf16[256,640]{1,0:T(8,128)(2,1)S(1)}, u32[]{:S(2)}, u32[]{:S(2)}) collective-permute-start(bf16[256,640]{1,0:T(8,128)(2,1)S(1)} %fusion.10), channel_id=1, source_target_pairs={{0,4},{2,6},{4,0},{6,2},{8,12},{10,14},{12,8},{14,10},{16,20},{18,... | collective-permute-start | bytes 983048 | tf_op jit(solution)/shard_map/ppermute | solution.py:61
  128.7 19.8 %collective-permute-start.23 = (bf16[2,2,352,384]{3,2,1,0:T(8,128)(2,1)}, bf16[2,2,352,384]{3,2,1,0:T(8,128)(2,1)S(1)}, u32[]{:S(2)}, u32[]{:S(2)}) collective-permute-start(bf16[2,2,352,384]{3,2,1,0:T(8,128)(2,1)} %get-tuple-element.211), channel_id=1, source_target_pairs={{0,2},{2,0},{4,6},{6,4},{8,10},{10,8},{12,14},{14,12},{16,18},{18,... | collective-permute-start | bytes 3244040 | tf_op jit(solution)/shard_map/ppermute | solution.py:58
  132.1 11.2 %collective-permute-start.30 = (bf16[2,160,512]{2,1,0:T(8,128)(2,1)S(1)}, bf16[2,160,512]{2,1,0:T(8,128)(2,1)S(1)}, u32[]{:S(2)}, u32[]{:S(2)}) collective-permute-start(bf16[2,160,512]{2,1,0:T(8,128)(2,1)S(1)} %fusion.15), channel_id=1, source_target_pairs={{0,1},{1,0},{2,3},{3,2},{4,5},{5,4},{6,7},{7,6},{8,9},{9,8},{10,11... | collective-permute-start | bytes 983048 | tf_op jit(solution)/shard_map/ppermute | solution.py:67
  137.6 10.9 %collective-permute-start.26 = (bf16[320,512]{1,0:T(8,128)(2,1)S(1)}, bf16[320,512]{1,0:T(8,128)(2,1)S(1)}, u32[]{:S(2)}, u32[]{:S(2)}) collective-permute-start(bf16[320,512]{1,0:T(8,128)(2,1)S(1)} %fusion.9), channel_id=1, source_target_pairs={{0,4},{2,6},{4,0},{6,2},{8,12},{10,14},{12,8},{14,10},{16,20},{18,... | collective-permute-start | bytes 983048 | tf_op jit(solution)/shard_map/ppermute | solution.py:61
  140.3 7.7 %collective-permute-start.27 = (bf16[64,640]{1,0:T(8,128)(2,1)S(1)}, bf16[64,640]{1,0:T(8,128)(2,1)S(1)}, u32[]{:S(2)}, u32[]{:S(2)}) collective-permute-start(bf16[64,640]{1,0:T(8,128)(2,1)S(1)} %get-tuple-element.350), channel_id=1, source_target_pairs={{0,8},{2,10},{4,12},{6,14},{8,16},{10,18},{12,20},{14,22},{16,24},... | collective-permute-start | bytes 245768 | tf_op jit(solution)/shard_map/ppermute | solution.py:64
  141.6 6.9 %collective-permute-start.28 = (bf16[64,640]{1,0:T(8,128)(2,1)S(1)}, bf16[64,640]{1,0:T(8,128)(2,1)S(1)}, u32[]{:S(2)}, u32[]{:S(2)}) collective-permute-start(bf16[64,640]{1,0:T(8,128)(2,1)S(1)} %get-tuple-element.349), channel_id=1, source_target_pairs={{0,16},{2,18},{4,20},{6,22},{8,24},{10,26},{12,28},{14,30},{16,0},... | collective-permute-start | bytes 245768 | tf_op jit(solution)/shard_map/ppermute | solution.py:64
  148.7 16.1 %collective-permute-start.32 = (bf16[480,512]{1,0:T(8,128)(2,1)S(1)}, bf16[480,512]{1,0:T(8,128)(2,1)S(1)}, u32[]{:S(2)}, u32[]{:S(2)}) collective-permute-start(bf16[480,512]{1,0:T(8,128)(2,1)S(1)} %pad_maximum_fusion), channel_id=1, source_target_pairs={{0,4},{2,6},{4,0},{6,2},{8,12},{10,14},{12,8},{14,10},{16,20},{18,... | collective-permute-start | bytes 1474568 | tf_op jit(solution)/shard_map/ppermute | solution.py:61
  150.0 14.8 %collective-permute-start.31 = (bf16[2,352,384]{2,1,0:T(8,128)(2,1)S(1)}, bf16[2,352,384]{2,1,0:T(8,128)(2,1)S(1)}, u32[]{:S(2)}, u32[]{:S(2)}) collective-permute-start(bf16[2,352,384]{2,1,0:T(8,128)(2,1)S(1)} %fusion.11), channel_id=1, source_target_pairs={{0,1},{1,0},{2,3},{3,2},{4,5},{5,4},{6,7},{7,6},{8,9},{9,8},{10,11... | collective-permute-start | bytes 1622024 | tf_op jit(solution)/shard_map/ppermute | solution.py:67
  157.8 6.5 %collective-permute-start.34 = (bf16[80,512]{1,0:T(8,128)(2,1)S(1)}, bf16[80,512]{1,0:T(8,128)(2,1)S(1)}, u32[]{:S(2)}, u32[]{:S(2)}) collective-permute-start(bf16[80,512]{1,0:T(8,128)(2,1)S(1)} %get-tuple-element.345), channel_id=1, source_target_pairs={{0,16},{2,18},{4,20},{6,22},{8,24},{10,26},{12,28},{14,30},{16,0},... | collective-permute-start | bytes 245768 | tf_op jit(solution)/shard_map/ppermute | solution.py:64
  164.9 6.2 %collective-permute-start.43 = (bf16[80,512]{1,0:T(8,128)(2,1)S(1)}, bf16[80,512]{1,0:T(8,128)(2,1)S(1)}, u32[]{:S(2)}, u32[]{:S(2)}) collective-permute-start(bf16[80,512]{1,0:T(8,128)(2,1)S(1)} %add_convert_fusion.7), channel_id=1, source_target_pairs={{0,8},{2,10},{4,12},{6,14},{8,16},{10,18},{12,20},{14,22},{16,24},... | collective-permute-start | bytes 245768 | tf_op jit(solution)/shard_map/ppermute | solution.py:64
  169.1 13.1 %collective-permute-start.46 = (bf16[256,640]{1,0:T(8,128)(2,1)S(1)}, bf16[256,640]{1,0:T(8,128)(2,1)S(1)}, u32[]{:S(2)}, u32[]{:S(2)}) collective-permute-start(bf16[256,640]{1,0:T(8,128)(2,1)S(1)} %bitcast.165), channel_id=1, source_target_pairs={{0,4},{2,6},{4,0},{6,2},{8,12},{10,14},{12,8},{14,10},{16,20},{18,... | collective-permute-start | bytes 983048 | tf_op jit(solution)/shard_map/ppermute | solution.py:61
  170.5 11.8 %collective-permute-start.39 = (bf16[352,384]{1,0:T(8,128)(2,1)S(1)}, bf16[352,384]{1,0:T(8,128)(2,1)S(1)}, u32[]{:S(2)}, u32[]{:S(2)}) collective-permute-start(bf16[352,384]{1,0:T(8,128)(2,1)S(1)} %fusion.12), channel_id=1, source_target_pairs={{0,4},{2,6},{4,0},{6,2},{8,12},{10,14},{12,8},{14,10},{16,20},{18,... | collective-permute-start | bytes 811016 | tf_op jit(solution)/shard_map/ppermute | solution.py:61
  172.7 9.5 %collective-permute-start.41 = (bf16[120,512]{1,0:T(8,128)(2,1)S(1)}, bf16[120,512]{1,0:T(8,128)(2,1)S(1)}, u32[]{:S(2)}, u32[]{:S(2)}) collective-permute-start(bf16[120,512]{1,0:T(8,128)(2,1)S(1)} %get-tuple-element.333), channel_id=1, source_target_pairs={{0,16},{2,18},{4,20},{6,22},{8,24},{10,26},{12,28},{14,30},{16,0},... | collective-permute-start | bytes 368648 | tf_op jit(solution)/shard_map/ppermute | solution.py:64
  173.1 9.2 %collective-permute-start.42 = (bf16[120,512]{1,0:T(8,128)(2,1)S(1)}, bf16[120,512]{1,0:T(8,128)(2,1)S(1)}, u32[]{:S(2)}, u32[]{:S(2)}) collective-permute-start(bf16[120,512]{1,0:T(8,128)(2,1)S(1)} %get-tuple-element.332), channel_id=1, source_target_pairs={{0,24},{2,26},{4,28},{6,30},{8,0},{10,2},{12,4},{14,6},{16,8},{18,... | collective-permute-start | bytes 368648 | tf_op jit(solution)/shard_map/ppermute | solution.py:64
  182.4 26.5 %collective-permute-start.53 = (bf16[320,512]{1,0:T(8,128)(2,1)S(1)}, bf16[320,512]{1,0:T(8,128)(2,1)S(1)}, u32[]{:S(2)}, u32[]{:S(2)}) collective-permute-start(bf16[320,512]{1,0:T(8,128)(2,1)S(1)} %bitcast.168), channel_id=1, source_target_pairs={{0,4},{2,6},{4,0},{6,2},{8,12},{10,14},{12,8},{14,10},{16,20},{18,... | collective-permute-start | bytes 983048 | tf_op jit(solution)/shard_map/ppermute | solution.py:61
  187.3 7.3 %collective-permute-start.48 = (bf16[88,384]{1,0:T(8,128)(2,1)S(1)}, bf16[88,384]{1,0:T(8,128)(2,1)S(1)}, u32[]{:S(2)}, u32[]{:S(2)}) collective-permute-start(bf16[88,384]{1,0:T(8,128)(2,1)S(1)} %get-tuple-element.357), channel_id=1, source_target_pairs={{0,16},{2,18},{4,20},{6,22},{8,24},{10,26},{12,28},{14,30},{16,0},... | collective-permute-start | bytes 202760 | tf_op jit(solution)/shard_map/ppermute | solution.py:64
  187.4 21.0 %collective-permute-start.50 = (bf16[120,512]{1,0:T(8,128)(2,1)S(1)}, bf16[120,512]{1,0:T(8,128)(2,1)S(1)}, u32[]{:S(2)}, u32[]{:S(2)}) collective-permute-start(bf16[120,512]{1,0:T(8,128)(2,1)S(1)} %add_convert_fusion.6), channel_id=1, source_target_pairs={{0,8},{2,10},{4,12},{6,14},{8,16},{10,18},{12,20},{14,22},{16,24},... | collective-permute-start | bytes 368648 | tf_op jit(solution)/shard_map/ppermute | solution.py:64
  187.5 20.9 %collective-permute-start.51 = (bf16[120,512]{1,0:T(8,128)(2,1)S(1)}, bf16[120,512]{1,0:T(8,128)(2,1)S(1)}, u32[]{:S(2)}, u32[]{:S(2)}) collective-permute-start(bf16[120,512]{1,0:T(8,128)(2,1)S(1)} %add_convert_fusion.6), channel_id=1, source_target_pairs={{0,16},{2,18},{4,20},{6,22},{8,24},{10,26},{12,28},{14,30},{16,0},... | collective-permute-start | bytes 368648 | tf_op jit(solution)/shard_map/ppermute | solution.py:64
  189.9 19.0 %collective-permute-start.52 = (bf16[120,512]{1,0:T(8,128)(2,1)S(1)}, bf16[120,512]{1,0:T(8,128)(2,1)S(1)}, u32[]{:S(2)}, u32[]{:S(2)}) collective-permute-start(bf16[120,512]{1,0:T(8,128)(2,1)S(1)} %add_convert_fusion.6), channel_id=1, source_target_pairs={{0,24},{2,26},{4,28},{6,30},{8,0},{10,2},{12,4},{14,6},{16,8},{18,... | collective-permute-start | bytes 368648 | tf_op jit(solution)/shard_map/ppermute | solution.py:64
  198.4 11.3 %collective-permute-start.67 = (bf16[256,640]{1,0:T(8,128)(2,1)S(1)}, bf16[256,640]{1,0:T(8,128)(2,1)S(1)}, u32[]{:S(2)}, u32[]{:S(2)}) collective-permute-start(bf16[256,640]{1,0:T(8,128)(2,1)S(1)} %bitcast.166), channel_id=1, source_target_pairs={{0,2},{2,0},{4,6},{6,4},{8,10},{10,8},{12,14},{14,12},{16,18},{18,... | collective-permute-start | bytes 983048 | tf_op jit(solution)/shard_map/ppermute | solution.py:58
  209.1 12.8 %collective-permute-start.54 = (bf16[480,512]{1,0:T(8,128)(2,1)S(1)}, bf16[480,512]{1,0:T(8,128)(2,1)S(1)}, u32[]{:S(2)}, u32[]{:S(2)}) collective-permute-start(bf16[480,512]{1,0:T(8,128)(2,1)S(1)} %bitcast.162), channel_id=1, source_target_pairs={{0,4},{2,6},{4,0},{6,2},{8,12},{10,14},{12,8},{14,10},{16,20},{18,... | collective-permute-start | bytes 1474568 | tf_op jit(solution)/shard_map/ppermute | solution.py:61
  209.2 29.2 %collective-permute-start.63 = (bf16[480,512]{1,0:T(8,128)(2,1)S(1)}, bf16[480,512]{1,0:T(8,128)(2,1)S(1)}, u32[]{:S(2)}, u32[]{:S(2)}) collective-permute-start(bf16[480,512]{1,0:T(8,128)(2,1)S(1)} %bitcast.163), channel_id=1, source_target_pairs={{0,2},{2,0},{4,6},{6,4},{8,10},{10,8},{12,14},{14,12},{16,18},{18,... | collective-permute-start | bytes 1474568 | tf_op jit(solution)/shard_map/ppermute | solution.py:58
  209.6 8.6 %collective-permute-start.57 = (bf16[88,384]{1,0:T(8,128)(2,1)S(1)}, bf16[88,384]{1,0:T(8,128)(2,1)S(1)}, u32[]{:S(2)}, u32[]{:S(2)}) collective-permute-start(bf16[88,384]{1,0:T(8,128)(2,1)S(1)} %add_convert_fusion.9), channel_id=1, source_target_pairs={{0,8},{2,10},{4,12},{6,14},{8,16},{10,18},{12,20},{14,22},{16,24},... | collective-permute-start | bytes 202760 | tf_op jit(solution)/shard_map/ppermute | solution.py:64
  213.6 6.1 %collective-permute-start.58 = (bf16[88,384]{1,0:T(8,128)(2,1)S(1)}, bf16[88,384]{1,0:T(8,128)(2,1)S(1)}, u32[]{:S(2)}, u32[]{:S(2)}) collective-permute-start(bf16[88,384]{1,0:T(8,128)(2,1)S(1)} %add_convert_fusion.9), channel_id=1, source_target_pairs={{0,16},{2,18},{4,20},{6,22},{8,24},{10,26},{12,28},{14,30},{16,0},... | collective-permute-start | bytes 202760 | tf_op jit(solution)/shard_map/ppermute | solution.py:64
  222.1 7.2 %collective-permute-start.60 = (bf16[352,384]{1,0:T(8,128)(2,1)S(1)}, bf16[352,384]{1,0:T(8,128)(2,1)S(1)}, u32[]{:S(2)}, u32[]{:S(2)}) collective-permute-start(bf16[352,384]{1,0:T(8,128)(2,1)S(1)} %bitcast.173), channel_id=1, source_target_pairs={{0,4},{2,6},{4,0},{6,2},{8,12},{10,14},{12,8},{14,10},{16,20},{18,... | collective-permute-start | bytes 811016 | tf_op jit(solution)/shard_map/ppermute | solution.py:61
  222.4 13.7 %collective-permute-start.55 = (bf16[256,640]{1,0:T(8,128)(2,1)S(1)}, bf16[256,640]{1,0:T(8,128)(2,1)S(1)}, u32[]{:S(2)}, u32[]{:S(2)}) collective-permute-start(bf16[256,640]{1,0:T(8,128)(2,1)S(1)} %get-tuple-element.326), channel_id=1, source_target_pairs={{1,0},{2,1},{3,2},{4,3},{5,4},{6,5},{7,6},{8,7},{9,8},{10,9},{11,1... | collective-permute-start | bytes 983048 | tf_op jit(solution)/shard_map/ppermute | solution.py:72
  225.9 11.6 %collective-permute-start.56 = (bf16[256,640]{1,0:T(8,128)(2,1)S(1)}, bf16[256,640]{1,0:T(8,128)(2,1)S(1)}, u32[]{:S(2)}, u32[]{:S(2)}) collective-permute-start(bf16[256,640]{1,0:T(8,128)(2,1)S(1)} %get-tuple-element.327), channel_id=1, source_target_pairs={{2,0},{3,1},{4,2},{5,3},{6,4},{7,5},{8,6},{9,7},{10,8},{11,9},{12,... | collective-permute-start | bytes 983048 | tf_op jit(solution)/shard_map/ppermute | solution.py:72
  227.8 10.5 %collective-permute-start.64 = (bf16[480,512]{1,0:T(8,128)(2,1)S(1)}, bf16[480,512]{1,0:T(8,128)(2,1)S(1)}, u32[]{:S(2)}, u32[]{:S(2)}) collective-permute-start(bf16[480,512]{1,0:T(8,128)(2,1)S(1)} %collective-permute-done.54), channel_id=1, source_target_pairs={{0,2},{2,0},{4,6},{6,4},{8,10},{10,8},{12,14},{14,12},{16,18},{18,... | collective-permute-start | bytes 1474568 | tf_op jit(solution)/shard_map/ppermute | solution.py:58
  229.3 12.7 %collective-permute-start.61 = (bf16[352,384]{1,0:T(8,128)(2,1)S(1)}, bf16[352,384]{1,0:T(8,128)(2,1)S(1)}, u32[]{:S(2)}, u32[]{:S(2)}) collective-permute-start(bf16[352,384]{1,0:T(8,128)(2,1)S(1)} %bitcast.175), channel_id=1, source_target_pairs={{0,2},{2,0},{4,6},{6,4},{8,10},{10,8},{12,14},{14,12},{16,18},{18,... | collective-permute-start | bytes 811016 | tf_op jit(solution)/shard_map/ppermute | solution.py:58
  (65 other events, 461.2 us)
